TPU v7x, 768 devices: a whole 4x8x12 slice. The times are simulated.
768 devices in a mesh: seq: 48 (over x, z), dp: 16 (over y, core).
Axes of the slice: x: 4, y: 8, z: 12, core: 2. Of those that a mesh axis runs over, the one named last changes fastest.
Arguments:
- features: bfloat16 [16, 12288, 768], P('dp', 'seq'), may hold values from -6 to 6
- feature_cot: bfloat16 [16, 12288, 768], P('dp', 'seq'), may hold values from -6 to 6
- depth_weight: bfloat16 [3, 768], replicated, may hold values from -3.5 to 3.5
- mix_weight: bfloat16 [768, 768], replicated, may hold values from -0.21875 to 0.21875
- tissue_scale: bfloat16 [184, 768], replicated, may hold values from -12 to 12
- donor_site: int32 [16, 3072], P('dp', 'seq'), may hold values from 0 to 255
- acceptor_hop: int32 [16, 3072, 1], P('dp', 'seq'), may hold values from 0 to 4; in each aligned block of 64 rows (0 to 63, 64 to 127, ..., all dimensions but the last counted through in order) at most 16 rows name the same one
- acceptor_site: int32 [16, 3072], P('dp', 'seq'), may hold values from 0 to 255
- live_count: int32 [16, 48], P('dp', 'seq'), may hold values from 8 to 64, as said below
- score_cot: bfloat16 [16, 184, 3072], P('dp', None, 'seq'), may hold values from -6 to 6
Outputs:
- junction_scores: float32 [16, 184, 3072], P('dp', None, 'seq')
- input_grad: bfloat16 [16, 12288, 768], P('dp', 'seq')
- conv_grad: float32 [589824], P(('seq', 'dp'))
- scale_grads: float32 [143616], P(('seq', 'dp'))
Inputs may be any that keep to these rules, and one draw needn't show every extreme that they name: Slots 0 to live_count - 1 of a shard hold junctions, the others are padding; in every sequence some shard has all 64 slots live. `acceptor_hop`: junctions whose acceptor shard falls outside the sequence are padding. Among the 64 slots of one shard no value occurs more than 16 times, and 16 is reached in some shard.
All inputs are finite; a program needn't handle non-finite values.
Results may differ from a plain program's by a relative error of at most 0.0083.
Values may be sent and summed in bfloat16 or wider, within the bound.
A program may use at most 32 MiB of HBM per device.

v0:
```python
import math

import jax
import jax.numpy as jnp
from jax import lax
from jax.sharding import PartitionSpec as P

REACH = 2
CAP = 16


def extended(cells, sides, width):
    for axis, dim in sides:
        count = lax.axis_size(axis)
        ends = count - 1
        head = lax.slice_in_dim(cells, 0, width, axis=dim)
        tail = lax.slice_in_dim(cells, cells.shape[dim] - width, cells.shape[dim], axis=dim)
        cells = jnp.concatenate(
            [
                lax.ppermute(tail, axis, [(i, (i + 1) % count) for i in range(ends)]),
                cells,
                lax.ppermute(head, axis, [((i + 1) % count, i) for i in range(ends)]),
            ],
            axis=dim,
        )
    return cells


def from_behind(block, axis, distance):
    devices = range(lax.axis_size(axis))
    route = [(i - distance, i) for i in devices if i - distance in devices]
    return lax.ppermute(block, axis, route)


def pair_terms(donor_rows, acceptor_rows, cotangent, alive_mask, tissue_scale, inv_root):
    pair_product = (donor_rows.astype(jnp.float32) * acceptor_rows.astype(jnp.float32)).astype(
        jnp.bfloat16
    )
    raw_score = (
        jnp.einsum("tc,mc->tm", tissue_scale, pair_product, preferred_element_type=jnp.float32)
        * inv_root
    )
    alive_float = alive_mask.astype(jnp.float32)
    scores = jax.nn.softplus(raw_score) * alive_float
    score_slope = (cotangent.astype(jnp.float32) * jax.nn.sigmoid(raw_score) * alive_float).astype(
        jnp.bfloat16
    )
    track_mix = jnp.einsum(
        "tm,tc->mc", score_slope, tissue_scale, preferred_element_type=jnp.float32
    )
    return (pair_product, scores, score_slope, track_mix)


def on_device(
    features,
    feature_cot,
    depth_weight,
    mix_weight,
    tissue_scale,
    donor_site,
    acceptor_hop,
    acceptor_site,
    live_count,
    score_cot,
):
    length = features.shape[1]
    channels = features.shape[2]
    tracks = tissue_scale.shape[0]
    slot_count = donor_site.shape[1]
    tap_count = depth_weight.shape[0]
    inv_root = 1.0 / math.sqrt(channels)
    shards = lax.axis_size("seq")
    data_ways = lax.axis_size("dp")
    position = lax.axis_index("seq")
    hop_count = 2 * REACH + 1
    bucket = CAP
    buffer_rows = hop_count * bucket
    depth_float = depth_weight.astype(jnp.float32)
    inputs = features[0]
    padded = extended(inputs, (("seq", 0),), 1)
    smooth_acc = padded[0:length].astype(jnp.float32) * depth_float[0]
    for offset in range(1, tap_count):
        smooth_acc = (
            smooth_acc + padded[offset : offset + length].astype(jnp.float32) * depth_float[offset]
        )
    smoothed = smooth_acc.astype(jnp.bfloat16)
    pre_act = jnp.dot(smoothed, mix_weight, preferred_element_type=jnp.float32)
    activated, gelu_back = jax.vjp(jax.nn.gelu, pre_act)
    embedding = activated.astype(jnp.bfloat16)
    hop_values = acceptor_hop[0, :, 0] - REACH
    slot_ids = jnp.arange(slot_count, dtype=jnp.int32)
    target = position + hop_values
    slot_live = (slot_ids < live_count[0, 0]) & (target >= 0) & (target < shards)
    hop_range = jnp.arange(hop_count, dtype=jnp.int32) - REACH
    member = (hop_values[:, None] == hop_range[None, :]) & slot_live[:, None]
    ranking = jnp.cumsum(member.astype(jnp.int32), axis=0) - 1
    chosen = member.T[:, None, :] & (
        ranking.T[:, None, :] == jnp.arange(bucket, dtype=jnp.int32)[None, :, None]
    )
    chosen_weight = chosen.astype(jnp.bfloat16)
    donor_rows = embedding[donor_site[0]]
    out_rows = jnp.einsum(
        "hks,sc->hkc", chosen_weight, donor_rows, preferred_element_type=jnp.float32
    ).astype(jnp.bfloat16)
    out_cot = jnp.einsum(
        "ts,hks->thk", score_cot[0], chosen_weight, preferred_element_type=jnp.float32
    ).astype(jnp.bfloat16)
    out_code = jnp.sum(jnp.where(chosen, acceptor_site[0][None, None, :] + 1, 0), axis=-1)
    home_index = jnp.sum(jnp.where(chosen, donor_site[0][None, None, :], 0), axis=-1).reshape(-1)
    home_live = jnp.any(chosen, axis=-1).reshape(-1)
    got_rows = []
    got_code = []
    got_cot = []
    for hop_index in range(hop_count):
        distance = hop_index - REACH
        parcel = (out_rows[hop_index], out_code[hop_index], out_cot[:, hop_index])
        if distance != 0:
            parcel = from_behind(
                (out_rows[hop_index], out_code[hop_index], out_cot[:, hop_index]), "seq", distance
            )
        got_rows.append(parcel[0])
        got_code.append(parcel[1])
        got_cot.append(parcel[2])
    in_rows = jnp.stack(got_rows).reshape(buffer_rows, channels)
    in_code = jnp.stack(got_code).reshape(buffer_rows)
    in_cot = jnp.stack(got_cot, axis=1).reshape(tracks, buffer_rows)
    in_live = in_code > 0
    in_index = jnp.maximum(in_code - 1, 0)
    acceptor_rows = embedding[in_index]
    pair_product, far_scores, score_slope, track_mix = pair_terms(
        in_rows, acceptor_rows, in_cot, in_live, tissue_scale, inv_root
    )
    live_column = in_live.astype(jnp.float32)[:, None]
    junction_grad = (
        jnp.zeros((length, channels), jnp.float32)
        .at[in_index]
        .add(track_mix * in_rows.astype(jnp.float32) * inv_root * live_column)
    )
    tissue_part = (
        jnp.einsum("tm,mc->tc", score_slope, pair_product, preferred_element_type=jnp.float32)
        * inv_root
    )
    donor_terms = (track_mix * acceptor_rows.astype(jnp.float32) * inv_root).reshape(
        hop_count, bucket, channels
    )
    score_blocks = far_scores.reshape(tracks, hop_count, bucket)
    back_terms = []
    back_scores = []
    for hop_index in range(hop_count):
        distance = hop_index - REACH
        parcel = (donor_terms[hop_index], score_blocks[:, hop_index])
        if distance != 0:
            parcel = from_behind(
                (donor_terms[hop_index], score_blocks[:, hop_index]), "seq", -distance
            )
        back_terms.append(parcel[0])
        back_scores.append(parcel[1])
    donor_grad = jnp.stack(back_terms).reshape(buffer_rows, channels)
    home_scores = jnp.stack(back_scores, axis=1)
    live_home = home_live.astype(jnp.float32)[:, None]
    junction_grad = junction_grad.at[home_index].add(donor_grad * live_home)
    slot_scores = jnp.einsum(
        "thk,hks->ts", home_scores, chosen.astype(jnp.float32), precision=lax.Precision.HIGHEST
    )
    total_grad = feature_cot[0].astype(jnp.float32) + junction_grad
    pre_slope = gelu_back(total_grad)[0].astype(jnp.bfloat16)
    smooth_slope = jnp.einsum(
        "lo,io->li", pre_slope, mix_weight, preferred_element_type=jnp.float32
    ).astype(jnp.bfloat16)
    padded_slope = extended(smooth_slope, (("seq", 0),), 1)
    input_grad = (
        padded_slope[tap_count - 1 : tap_count - 1 + length].astype(jnp.float32) * depth_float[0]
    )
    for offset in range(1, tap_count):
        begin_row = tap_count - 1 - offset
        input_grad = (
            input_grad
            + padded_slope[begin_row : begin_row + length].astype(jnp.float32) * depth_float[offset]
        )
    slope_float = smooth_slope.astype(jnp.float32)
    depth_part = jnp.stack(
        [
            jnp.sum(padded[offset : offset + length].astype(jnp.float32) * slope_float, axis=0)
            for offset in range(tap_count)
        ]
    )
    mix_part = jnp.einsum("li,lo->io", smoothed, pre_slope, preferred_element_type=jnp.float32)
    grad_scale = 1.0 / math.sqrt(length * shards * data_ways)
    mix_flat = mix_part.reshape(-1)
    head_flat = jnp.concatenate([tissue_part.reshape(-1), depth_part.reshape(-1) * grad_scale])
    mix_share, head_share = (
        lax.psum_scatter(mix_flat, ("seq", "dp"), scatter_dimension=0, tiled=True),
        lax.psum_scatter(head_flat, ("seq", "dp"), scatter_dimension=0, tiled=True),
    )
    return (
        slot_scores[None],
        input_grad.astype(jnp.bfloat16)[None],
        mix_share * grad_scale,
        head_share.reshape(-1),
    )


def solution(mesh):
    placed = (
        P("dp", "seq", None),
        P("dp", "seq", None),
        P(),
        P(),
        P(),
        P("dp", "seq"),
        P("dp", "seq", None),
        P("dp", "seq"),
        P("dp", "seq"),
        P("dp", None, "seq"),
    )
    return jax.shard_map(
        on_device,
        mesh=mesh,
        in_specs=placed,
        out_specs=(P("dp", None, "seq"), P("dp", "seq", None), P(("seq", "dp")), P(("seq", "dp"))),
        check_vma=False,
    )
```

profile of v0, /device:TPU:1, one launch (start us, length us, event | category | flops | bytes accessed | tf_op | source)
XLA Modules:
  0.0 625.5 jit_solution(14872274609528610080)
XLA Ops:
  7.3 0.8 add_bitcast_fusion.2
  8.7 0.7 compare_and_fusion.1
  9.7 0.9 fusion.1
  10.6 1.3 collective-permute-start.14
  11.9 1.3 collective-permute-start.15
  13.2 0.7 add_bitcast_fusion.1
  13.8 0.9 select_reduce_fusion
  14.7 1.3 collective-permute-start.6
  16.0 1.3 collective-permute-start.7
  17.3 6.1 collective-permute-start.8
  23.4 0.7 fusion.42
  24.3 0.7 slice_bitcast_fusion.14
  25.0 0.7 convert_element_type.110
  25.8 1.1 bitcast_convert_fusion
  26.9 0.6 fusion.43
  27.5 0.7 reshape.228
  28.2 7.1 %collective-permute-start.9 = (s32[16]{0:T(128)S(1)}, s32[16]{0:T(128)S(1)}, u32[]{:S(2)}, u32[]{:S(2)}) collective-permute-start(s32[16]{0:T(128)S(1)} %get-tuple-element.42), channel_id=1, source_target_pairs={{0,32},{16,48},{32,64},{48,80},{64,96},{80,112},{96,128},{112,144}... | collective-permute-start | bytes 200 | tf_op jit(solution)/shard_map/ppermute | solution.py:32
  35.3 1.3 collective-permute-start.1
  36.6 5.8 collective-permute-start
  42.6 0.5 copy-done.14
  43.1 0.6 mul.207
  43.8 1.6 multiply_convert_fusion
  45.4 0.7 gather_fusion
  46.3 4.0 collective-permute-start.16
  50.4 0.7 gather_fusion.1
  51.1 1.3 collective-permute-start.2
  52.4 1.3 collective-permute-start.3
  53.7 7.6 %collective-permute-start.17 = (bf16[184,16]{0,1:T(8,128)(2,1)S(1)}, bf16[184,16]{0,1:T(8,128)(2,1)S(1)}, u32[]{:S(2)}, u32[]{:S(2)}) collective-permute-start(bf16[184,16]{0,1:T(8,128)(2,1)S(1)} %get-tuple-element.37), channel_id=1, source_target_pairs={{0,32},{16,48},{32,64},{48,80},{64,96},{80,112},{96,128},{112,144}... | collective-permute-start | bytes 17672 | tf_op jit(solution)/shard_map/ppermute | solution.py:32
  61.4 4.5 collective-permute-start.4
  65.9 5.5 collective-permute-start.5
  71.4 0.9 collective-permute-done.5
  72.4 0.9 fusion.28
  73.6 4.6 collective-permute-start.18
  78.2 0.3 convolution_multiply_fusion
  78.4 4.6 collective-permute-start.19
  83.0 1.3 collective-permute-start.20
  84.3 1.3 collective-permute-start.21
  85.6 0.9 reshape.223
  86.5 1.6 scatter_custom_fusion
  88.2 4.1 collective-permute-done.21
  92.3 0.8 bitcast_multiply_fusion
  93.0 1.7 scatter_fusion
  94.7 0.5 fusion.11
  95.3 0.5 convolution_convert_fusion
  95.8 0.7 fusion.48
  96.5 3.9 collective-permute-start.23
  100.5 1.3 collective-permute-start.22
  101.8 0.7 fusion.44
  102.5 1.6 reshape.222
  104.1 2.2 collective-permute-done.22
  106.3 3.2 fusion.15
  109.6 0.8 pad_maximum_fusion
  110.4 0.9 copy-done.7
  111.3 5.7 collective-permute-start.10
  117.0 4.6 collective-permute-start.11
  121.6 0.8 collective-permute-done.11
  122.5 1.3 collective-permute-start.12
  123.8 1.3 collective-permute-start.13
  125.1 2.2 collective-permute-done.12
  127.2 3.1 collective-permute-done.13
  130.3 0.9 convolution_bitcast_fusion
  131.2 484.8 %all-reduce.5.cloned.1.call-done = (f32[589824]{0:T(1024)}, f32[143616]{0:T(1024)}) async-done(((f32[589824]{0:T(1024)}, f32[143616]{0:T(1024)}), (f32[589824]{0:T(1024)}, f32[143616]{0:T(1024)})) %all-reduce.5.cloned.1.call-update) | async-done | bytes 2933776
  616.0 1.4 dynamic-slice_multiply_fusion
  617.3 1.3 dynamic-slice.1
  (99 shorter events, 1.6 us)
Async XLA Ops:
  7.2 36.6 %copy-start = (bf16[768,768]{1,0:T(8,128)(2,1)S(1)}, bf16[768,768]{1,0:T(8,128)(2,1)}, u32[]{:S(2)}) copy-start(bf16[768,768]{1,0:T(8,128)(2,1)} %param.13) | copy-start | bytes 3538948
  7.2 36.6 %copy-start.2 = (bf16[1,256,768]{2,1,0:T(8,128)(2,1)S(1)}, bf16[1,256,768]{2,1,0:T(8,128)(2,1)}, u32[]{:S(2)}) copy-start(bf16[1,256,768]{2,1,0:T(8,128)(2,1)} %param.10) | copy-start | bytes 1179652
  7.2 608.8 %all-reduce.5.cloned.1.call-start = ((), (), s32[]{:S(2)}) async-start(), calls=%async_computation | async-start | bytes 5873664
  10.6 35.7 %collective-permute-start.14 = (bf16[184,16]{0,1:T(8,128)(2,1)S(1)}, bf16[184,16]{0,1:T(8,128)(2,1)S(1)}, u32[]{:S(2)}, u32[]{:S(2)}) collective-permute-start(bf16[184,16]{0,1:T(8,128)(2,1)S(1)} %get-tuple-element.41), channel_id=1, source_target_pairs={{32,0},{48,16},{64,32},{80,48},{96,64},{112,80},{128,96},{144,112}... | collective-permute-start | bytes 17672 | tf_op jit(solution)/shard_map/ppermute | solution.py:32
  11.9 34.4 %collective-permute-start.15 = (bf16[184,16]{0,1:T(8,128)(2,1)S(1)}, bf16[184,16]{0,1:T(8,128)(2,1)S(1)}, u32[]{:S(2)}, u32[]{:S(2)}) collective-permute-start(bf16[184,16]{0,1:T(8,128)(2,1)S(1)} %get-tuple-element.40), channel_id=1, source_target_pairs={{16,0},{32,16},{48,32},{64,48},{80,64},{96,80},{112,96},{128,112},... | collective-permute-start | bytes 17672 | tf_op jit(solution)/shard_map/ppermute | solution.py:32
  14.7 13.4 %collective-permute-start.6 = (s32[16]{0:T(128)S(1)}, s32[16]{0:T(128)S(1)}, u32[]{:S(2)}, u32[]{:S(2)}) collective-permute-start(s32[16]{0:T(128)S(1)} %get-tuple-element.46), channel_id=1, source_target_pairs={{32,0},{48,16},{64,32},{80,48},{96,64},{112,80},{128,96},{144,112}... | collective-permute-start | bytes 200 | tf_op jit(solution)/shard_map/ppermute | solution.py:32
  16.0 19.2 %collective-permute-start.7 = (s32[16]{0:T(128)S(1)}, s32[16]{0:T(128)S(1)}, u32[]{:S(2)}, u32[]{:S(2)}) collective-permute-start(s32[16]{0:T(128)S(1)} %get-tuple-element.45), channel_id=1, source_target_pairs={{16,0},{32,16},{48,32},{64,48},{80,64},{96,80},{112,96},{128,112},... | collective-permute-start | bytes 200 | tf_op jit(solution)/shard_map/ppermute | solution.py:32
  17.3 19.2 %collective-permute-start.8 = (s32[16]{0:T(128)S(1)}, s32[16]{0:T(128)S(1)}, u32[]{:S(2)}, u32[]{:S(2)}) collective-permute-start(s32[16]{0:T(128)S(1)} %get-tuple-element.43), channel_id=1, source_target_pairs={{0,16},{16,32},{32,48},{48,64},{64,80},{80,96},{96,112},{112,128},... | collective-permute-start | bytes 200 | tf_op jit(solution)/shard_map/ppermute | solution.py:32
  25.8 20.3 %copy-start.8 = (f32[768]{0:T(1024)}, f32[768]{0:T(1024)S(1)}, u32[]{:S(2)}) copy-start(f32[768]{0:T(1024)S(1)} %get-tuple-element.9) | copy-start | bytes 9220
  28.2 14.2 %collective-permute-start.9 = (s32[16]{0:T(128)S(1)}, s32[16]{0:T(128)S(1)}, u32[]{:S(2)}, u32[]{:S(2)}) collective-permute-start(s32[16]{0:T(128)S(1)} %get-tuple-element.42), channel_id=1, source_target_pairs={{0,32},{16,48},{32,64},{48,80},{64,96},{80,112},{96,128},{112,144}... | collective-permute-start | bytes 200 | tf_op jit(solution)/shard_map/ppermute | solution.py:32
  35.3 8.5 %collective-permute-start.1 = (bf16[1,768]{1,0:T(2,128)(2,1)S(1)}, bf16[1,768]{1,0:T(2,128)(2,1)S(1)}, u32[]{:S(2)}, u32[]{:S(2)}) collective-permute-start(bf16[1,768]{1,0:T(2,128)(2,1)S(1)} %get-tuple-element.20), channel_id=1, source_target_pairs={{16,0},{32,16},{48,32},{64,48},{80,64},{96,80},{112,96},{128,112},... | collective-permute-start | bytes 4616 | tf_op jit(solution)/shard_map/ppermute | solution.py:22
  36.6 7.2 %collective-permute-start = (bf16[1,768]{1,0:T(2,128)(2,1)S(1)}, bf16[1,768]{1,0:T(2,128)(2,1)S(1)}, u32[]{:S(2)}, u32[]{:S(2)}) collective-permute-start(bf16[1,768]{1,0:T(2,128)(2,1)S(1)} %get-tuple-element.19), channel_id=1, source_target_pairs={{0,16},{16,32},{32,48},{48,64},{64,80},{80,96},{96,112},{112,128},... | collective-permute-start | bytes 4616 | tf_op jit(solution)/shard_map/ppermute | solution.py:20
  42.5 0.5 copy-start.14
  43.7 7.4 %copy-start.10 = (bf16[1,768]{1,0:T(2,128)(2,1)}, bf16[1,768]{1,0:T(2,128)(2,1)S(1)}, u32[]{:S(2)}) copy-start(bf16[1,768]{1,0:T(2,128)(2,1)S(1)} %collective-permute-done.1) | copy-start | bytes 4612
  43.7 1.6 copy-start.12
  46.1 26.3 %copy-start.6 = (bf16[184,768]{1,0:T(8,128)(2,1)S(1)}, bf16[184,768]{1,0:T(8,128)(2,1)}, u32[]{:S(2)}) copy-start(bf16[184,768]{1,0:T(8,128)(2,1)} %param.14) | copy-start | bytes 847876
  46.3 15.0 %collective-permute-start.16 = (bf16[184,16]{0,1:T(8,128)(2,1)S(1)}, bf16[184,16]{0,1:T(8,128)(2,1)S(1)}, u32[]{:S(2)}, u32[]{:S(2)}) collective-permute-start(bf16[184,16]{0,1:T(8,128)(2,1)S(1)} %get-tuple-element.38), channel_id=1, source_target_pairs={{0,16},{16,32},{32,48},{48,64},{64,80},{80,96},{96,112},{112,128},... | collective-permute-start | bytes 17672 | tf_op jit(solution)/shard_map/ppermute | solution.py:32
  51.1 10.3 %collective-permute-start.2 = (bf16[16,768]{1,0:T(8,128)(2,1)S(1)}, bf16[16,768]{1,0:T(8,128)(2,1)S(1)}, u32[]{:S(2)}, u32[]{:S(2)}) collective-permute-start(bf16[16,768]{1,0:T(8,128)(2,1)S(1)} %get-tuple-element.29), channel_id=1, source_target_pairs={{32,0},{48,16},{64,32},{80,48},{96,64},{112,80},{128,96},{144,112}... | collective-permute-start | bytes 73736 | tf_op jit(solution)/shard_map/ppermute | solution.py:32
  52.4 9.0 %collective-permute-start.3 = (bf16[16,768]{1,0:T(8,128)(2,1)S(1)}, bf16[16,768]{1,0:T(8,128)(2,1)S(1)}, u32[]{:S(2)}, u32[]{:S(2)}) collective-permute-start(bf16[16,768]{1,0:T(8,128)(2,1)S(1)} %get-tuple-element.28), channel_id=1, source_target_pairs={{16,0},{32,16},{48,32},{64,48},{80,64},{96,80},{112,96},{128,112},... | collective-permute-start | bytes 73736 | tf_op jit(solution)/shard_map/ppermute | solution.py:32
  53.7 12.2 %collective-permute-start.17 = (bf16[184,16]{0,1:T(8,128)(2,1)S(1)}, bf16[184,16]{0,1:T(8,128)(2,1)S(1)}, u32[]{:S(2)}, u32[]{:S(2)}) collective-permute-start(bf16[184,16]{0,1:T(8,128)(2,1)S(1)} %get-tuple-element.37), channel_id=1, source_target_pairs={{0,32},{16,48},{32,64},{48,80},{64,96},{80,112},{96,128},{112,144}... | collective-permute-start | bytes 17672 | tf_op jit(solution)/shard_map/ppermute | solution.py:32
  61.4 10.0 %collective-permute-start.4 = (bf16[16,768]{1,0:T(8,128)(2,1)S(1)}, bf16[16,768]{1,0:T(8,128)(2,1)S(1)}, u32[]{:S(2)}, u32[]{:S(2)}) collective-permute-start(bf16[16,768]{1,0:T(8,128)(2,1)S(1)} %get-tuple-element.26), channel_id=1, source_target_pairs={{0,16},{16,32},{32,48},{48,64},{64,80},{80,96},{96,112},{112,128},... | collective-permute-start | bytes 73736 | tf_op jit(solution)/shard_map/ppermute | solution.py:32
  65.9 6.4 %collective-permute-start.5 = (bf16[16,768]{1,0:T(8,128)(2,1)S(1)}, bf16[16,768]{1,0:T(8,128)(2,1)S(1)}, u32[]{:S(2)}, u32[]{:S(2)}) collective-permute-start(bf16[16,768]{1,0:T(8,128)(2,1)S(1)} %get-tuple-element.25), channel_id=1, source_target_pairs={{0,32},{16,48},{32,64},{48,80},{64,96},{80,112},{96,128},{112,144}... | collective-permute-start | bytes 73736 | tf_op jit(solution)/shard_map/ppermute | solution.py:32
  73.6 14.5 %collective-permute-start.18 = (f32[16,768]{1,0:T(8,128)S(1)}, f32[16,768]{1,0:T(8,128)S(1)}, u32[]{:S(2)}, u32[]{:S(2)}) collective-permute-start(f32[16,768]{1,0:T(8,128)S(1)} %get-tuple-element.24), channel_id=1, source_target_pairs={{0,32},{16,48},{32,64},{48,80},{64,96},{80,112},{96,128},{112,144}... | collective-permute-start | bytes 147464 | tf_op jit(solution)/shard_map/ppermute | solution.py:32
  78.4 9.7 %collective-permute-start.19 = (f32[16,768]{1,0:T(8,128)S(1)}, f32[16,768]{1,0:T(8,128)S(1)}, u32[]{:S(2)}, u32[]{:S(2)}) collective-permute-start(f32[16,768]{1,0:T(8,128)S(1)} %get-tuple-element.23), channel_id=1, source_target_pairs={{0,16},{16,32},{32,48},{48,64},{64,80},{80,96},{96,112},{112,128},... | collective-permute-start | bytes 147464 | tf_op jit(solution)/shard_map/ppermute | solution.py:32
  83.0 5.2 collective-permute-start.20
  84.3 8.0 %collective-permute-start.21 = (f32[16,768]{1,0:T(8,128)S(1)}, f32[16,768]{1,0:T(8,128)S(1)}, u32[]{:S(2)}, u32[]{:S(2)}) collective-permute-start(f32[16,768]{1,0:T(8,128)S(1)} %get-tuple-element.21), channel_id=1, source_target_pairs={{32,0},{48,16},{64,32},{80,48},{96,64},{112,80},{128,96},{144,112}... | collective-permute-start | bytes 147464 | tf_op jit(solution)/shard_map/ppermute | solution.py:32
  93.0 1.7 copy-start.5
  95.3 6.5 %copy-start.3 = (bf16[1,256,768]{2,1,0:T(8,128)(2,1)S(1)}, bf16[1,256,768]{2,1,0:T(8,128)(2,1)}, u32[]{:S(2)}) copy-start(bf16[1,256,768]{2,1,0:T(8,128)(2,1)} %param.10) | copy-start | bytes 1179652
  95.3 6.5 %copy-start.9 = (f32[768]{0:T(1024)S(1)}, f32[768]{0:T(1024)}, u32[]{:S(2)}) copy-start(f32[768]{0:T(1024)} %copy-done.8) | copy-start | bytes 9220
  95.3 6.5 %copy-start.11 = (bf16[1,768]{1,0:T(2,128)(2,1)S(1)}, bf16[1,768]{1,0:T(2,128)(2,1)}, u32[]{:S(2)}) copy-start(bf16[1,768]{1,0:T(2,128)(2,1)} %copy-done.10) | copy-start | bytes 4612
  95.3 6.5 %copy-start.13 = (bf16[1,768]{1,0:T(2,128)(2,1)S(1)}, bf16[1,768]{1,0:T(2,128)(2,1)}, u32[]{:S(2)}) copy-start(bf16[1,768]{1,0:T(2,128)(2,1)} %copy-done.12) | copy-start | bytes 4612
  95.8 4.6 copy-start.4
  96.5 7.6 %collective-permute-start.23 = (bf16[1,768]{1,0:T(2,128)(2,1)}, bf16[1,768]{1,0:T(2,128)(2,1)}, u32[]{:S(2)}, u32[]{:S(2)}) collective-permute-start(bf16[1,768]{1,0:T(2,128)(2,1)} %get-tuple-element.18), channel_id=1, source_target_pairs={{0,16},{16,32},{32,48},{48,64},{64,80},{80,96},{96,112},{112,128},... | collective-permute-start | bytes 4616 | tf_op jit(solution)/shard_map/ppermute | solution.py:20
  100.5 5.8 collective-permute-start.22
  104.1 5.5 copy-start.1
  110.4 0.9 copy-start.7
  111.3 10.3 %collective-permute-start.10 = (f32[184,16]{0,1:T(8,128)S(1)}, f32[184,16]{0,1:T(8,128)S(1)}, u32[]{:S(2)}, u32[]{:S(2)}) collective-permute-start(f32[184,16]{0,1:T(8,128)S(1)} %get-tuple-element.36), channel_id=1, source_target_pairs={{0,32},{16,48},{32,64},{48,80},{64,96},{80,112},{96,128},{112,144}... | collective-permute-start | bytes 35336 | tf_op jit(solution)/shard_map/ppermute | solution.py:32
  117.0 5.4 collective-permute-start.11
  122.5 4.7 collective-permute-start.12
  123.8 6.6 %collective-permute-start.13 = (f32[184,16]{0,1:T(8,128)S(1)}, f32[184,16]{0,1:T(8,128)S(1)}, u32[]{:S(2)}, u32[]{:S(2)}) collective-permute-start(f32[184,16]{0,1:T(8,128)S(1)} %get-tuple-element.32), channel_id=1, source_target_pairs={{32,0},{48,16},{64,32},{80,48},{96,64},{112,80},{128,96},{144,112}... | collective-permute-start | bytes 35336 | tf_op jit(solution)/shard_map/ppermute | solution.py:32
Sparse Core Ops, SparseCore 0:
  110.6 505.3 all-reduce.4
where the time goes:
time: 627 us; the launch traced here: 625 us
  waiting for transfers between devices  498 us (79%)
  starting transfers between devices  79.5 us (13%)
  other arithmetic  16.5 us (3%)
  between operations  15.5 us (2%)
  local copies, waits for them, and re-layouts  9.82 us (2%)
    unnamed x2, waiting for transfers between devices  485 us
    ppermute x20, starting transfers between devices, from_behind(): return lax.ppermute(block, axis, route)  67.1 us
  transfers between devices with their start and end apart: 25, of which 7 were waited for; matrix products, arithmetic and copies ran while one was open for 3% of the time, Pallas kernels for 0%

commit v1 on v0

v1 whole, which is shorter than its diff:
```python
import math

import jax
import jax.numpy as jnp
from jax import lax
from jax.experimental import pallas as pl
from jax.experimental.pallas import tpu as pltpu
from jax.sharding import PartitionSpec as P

F32 = jnp.float32
BF16 = jnp.bfloat16
MESH = pl.DeviceIdType.MESH

REACH = 2
HOPS = 2 * REACH + 1
CAP = 16
NX, NZ, NY, NC = 4, 12, 8, 2
SHARDS = NX * NZ
ROWS = 256
CH = 768
HALF = CH // 2
TRACKS = 184
HEAD = TRACKS + 3
HEAD_PAD = 192
SLOTS = 64
BUCKET = HOPS * CAP
XROWS = CH // NX
TROWS = 48
ZROWS = XROWS // NZ
SHARE = HEAD * CH // (SHARDS * NY * NC)

S_CODE, S_ROWS, S_FEAT, S_SLOPE = 0, 5, 10, 12
S_SMOOTH, S_PRE, S_HEAD, S_END = 14, 15, 16, 17
S_XM, S_XT, S_Z, S_Y = 18, 21, 24, 35
S_ALL = 42


def dot(a, b, left=1, right=0):
    return lax.dot_general(
        a, b, (((left,), (right,)), ((), ())), preferred_element_type=F32
    )


def iota(shape, dim):
    return lax.broadcasted_iota(jnp.int32, shape, dim).astype(F32)


def quotient(value, divisor):
    return jnp.floor((value + 0.5) * (1.0 / divisor))


def body(
    feat,
    fcot,
    taps,
    mix,
    scale,
    donor,
    hop,
    acceptor,
    live,
    cot,
    scores_out,
    grad_out,
    conv_out,
    head_out,
    code_out,
    code_in,
    rows_out,
    rows_in,
    halo_in,
    edge_out,
    edge_in,
    fpad,
    spad,
    act,
    emb,
    smooth,
    smooth_in,
    pre,
    pre_in,
    head,
    head_cast,
    head_in,
    xm_out,
    xm_own,
    xm_in,
    xt_out,
    xt_in,
    z_out,
    z_in,
    y_out,
    y_in,
    end_out,
    end_in,
    send,
    recv,
):
    seq = lax.axis_index("seq")
    dp = lax.axis_index("dp")
    x, z = lax.div(seq, NZ), lax.rem(seq, NZ)
    y, core = lax.div(dp, NC), lax.rem(dp, NC)
    inv_root = 1.0 / math.sqrt(CH)
    grad_scale = 1.0 / math.sqrt(ROWS * SHARDS * NY * NC)

    def along_seq(step):
        return {"seq": lax.rem(seq + SHARDS + step, SHARDS), "dp": dp}

    def along_x(step):
        return {"seq": lax.rem(x + step, NX) * NZ + z, "dp": dp}

    def along_z(step):
        return {"seq": x * NZ + lax.rem(z + step, NZ), "dp": dp}

    def along_y(step):
        return {"seq": seq, "dp": lax.rem(y + step, NY) * NC + core}

    partner = {"seq": seq, "dp": y * NC + 1 - core}

    def remote(src, dst, number, device):
        return pltpu.make_async_remote_copy(
            src_ref=src,
            dst_ref=dst,
            send_sem=send.at[number],
            recv_sem=recv.at[number],
            device_id=device,
            device_id_type=MESH,
        )

    barrier = pltpu.get_barrier_semaphore()

    def greet(device):
        pl.semaphore_signal(barrier, inc=1, device_id=device, device_id_type=MESH)

    for step in (-2, -1, 1, 2):
        greet(along_seq(step))
    greet(partner)
    for step in range(1, NX):
        greet(along_x(step))

    @pl.loop(1, NZ)
    def _(step):
        greet(along_z(step))

    @pl.loop(1, NY)
    def _(step):
        greet(along_y(step))

    hop_row = hop[...].astype(F32)
    seq_f = seq.astype(F32)
    target = hop_row + (seq_f - REACH)
    slot_row = iota((1, SLOTS), 1)
    live_f = live[...].astype(F32)
    live_row = (slot_row < live_f) & (target >= 0.0) & (target < float(SHARDS))
    key_row = jnp.where(live_row, hop_row, 7.0)
    eye = iota((SLOTS, SLOTS), 0) == iota((SLOTS, SLOTS), 1)

    def column(row):
        return jnp.sum(jnp.where(eye, row, 0.0), axis=1, keepdims=True)

    key_col = column(key_row)
    before = iota((SLOTS, SLOTS), 0) < iota((SLOTS, SLOTS), 1)
    rank_row = jnp.sum(
        jnp.where((key_col == key_row) & before, 1.0, 0.0), axis=0, keepdims=True
    )
    rank_col = column(rank_row)
    place = iota((BUCKET, SLOTS), 0)
    place_hop = quotient(place, CAP)
    chosen = (key_row == place_hop) & (rank_row == place - CAP * place_hop)
    chosen = jnp.where(chosen, 1.0, 0.0).astype(BF16)
    place = iota((SLOTS, BUCKET), 1)
    place_hop = quotient(place, CAP)
    unchosen = (key_col == place_hop) & (rank_col == place - CAP * place_hop)
    unchosen = jnp.where(unchosen, 1.0, 0.0).astype(BF16)
    live_col = jnp.where(key_col < 6.0, 1.0, 0.0)
    donor_col = column(donor[...].astype(F32))
    donor_hot = jnp.where(
        (iota((SLOTS, ROWS), 1) == donor_col) & (key_col < 6.0), 1.0, 0.0
    ).astype(BF16)
    code_col = column(acceptor[...].astype(F32)) + 1.0
    code_wide = jnp.broadcast_to(code_col, (SLOTS, 128)).astype(BF16)
    bucket_cot = dot(chosen, cot[...])
    bucket_code = dot(chosen, code_wide)
    parcel = jnp.concatenate(
        [bucket_cot, jnp.zeros((BUCKET, 256 - TRACKS), F32), bucket_code], axis=1
    ).astype(BF16)
    for h in range(HOPS):
        code_out[h] = parcel[h * CAP : (h + 1) * CAP]
    code_in[REACH] = parcel[REACH * CAP : (REACH + 1) * CAP]
    bucket_hot = dot(chosen, donor_hot).astype(BF16)

    fpad[8 : 8 + ROWS, :] = feat[...].astype(F32)

    pl.semaphore_wait(barrier, 4 + 1 + (NX - 1) + (NZ - 1) + (NY - 1))

    others = [h for h in range(HOPS) if h != REACH]
    feat_right = remote(feat.at[pl.ds(ROWS - 16, 16)], halo_in.at[0], S_FEAT, along_seq(1))
    feat_left = remote(feat.at[pl.ds(0, 16)], halo_in.at[1], S_FEAT + 1, along_seq(-1))
    feat_right.start()
    feat_left.start()
    code_copies = [
        remote(code_out.at[h], code_in.at[h], S_CODE + h, along_seq(h - REACH)) for h in others
    ]
    for copy in code_copies:
        copy.start()

    feat_right.wait_recv()
    feat_left.wait_recv()
    inner_low = jnp.where(seq > 0, 1.0, 0.0)
    inner_high = jnp.where(seq < SHARDS - 1, 1.0, 0.0)
    fpad[0:8, :] = halo_in[0].astype(F32)[8:16] * inner_low
    fpad[8 + ROWS : 16 + ROWS, :] = halo_in[1].astype(F32)[0:8] * inner_high
    tap = [taps[k : k + 1, :].astype(F32) for k in range(3)]
    step_rows = 32
    for at in range(0, ROWS, step_rows):
        total = fpad[at + 7 : at + 7 + step_rows, :] * tap[0]
        total = total + fpad[at + 8 : at + 8 + step_rows, :] * tap[1]
        total = total + fpad[at + 9 : at + 9 + step_rows, :] * tap[2]
        emb[at : at + step_rows, :] = total.astype(BF16)
    smoothed = emb[...]
    act[...] = dot(smoothed, mix[...])
    turned = smoothed.T
    for k in range(NX):
        smooth[k] = turned[k * XROWS : (k + 1) * XROWS]
    smooth_copy = remote(smooth, smooth_in, S_SMOOTH, partner)
    smooth_copy.start()

    root = math.sqrt(2.0 / math.pi)

    @pl.loop(0, ROWS // step_rows)
    def _(i):
        at = pl.ds(pl.multiple_of(i * step_rows, step_rows), step_rows)
        v = act[at, :]
        sq = v * v
        t = jnp.tanh(root * (v + 0.044715 * (sq * v)))
        emb[at, :] = (0.5 * v * (1.0 + t)).astype(BF16)
        act[at, :] = 0.5 * (1.0 + t) + (0.5 * root) * v * (1.0 - t * t) * (
            1.0 + (3.0 * 0.044715) * sq
        )

    for copy in code_copies:
        copy.wait_recv()
    codes = code_in[...].reshape(BUCKET, 384)
    in_cot = codes[:, :TRACKS].astype(F32)
    in_code = codes[:, 256:384].astype(F32) - 1.0
    lanes = iota((BUCKET, 128), 1)
    in_hot = jnp.concatenate(
        [
            jnp.where(in_code == lanes, 1.0, 0.0),
            jnp.where(in_code == lanes + 128.0, 1.0, 0.0),
        ],
        axis=1,
    ).astype(BF16)
    hot = jnp.concatenate([in_hot, donor_hot, bucket_hot], axis=0)
    picked = dot(hot, emb[...]).astype(BF16)
    both = BUCKET + SLOTS
    own_rows = picked[:both]
    here = picked[:BUCKET]
    there = picked[both:]
    for h in range(HOPS):
        back = HOPS - 1 - h
        rows_out[h, 0:CAP, :] = there[h * CAP : (h + 1) * CAP]
        rows_out[h, CAP : 2 * CAP, :] = here[back * CAP : (back + 1) * CAP]
    rows_in[REACH] = rows_out[REACH]
    rows_copies = [
        remote(rows_out.at[h], rows_in.at[h], S_ROWS + h, along_seq(h - REACH)) for h in others
    ]
    for copy in rows_copies:
        copy.start()

    spread = hot[:both].T

    z_place = iota((XROWS, 3 * TROWS), 0)
    z_to = quotient(z_place, ZROWS)
    z_chunk = z_place - ZROWS * z_to
    z_tile = quotient(z_chunk, 5)
    x_f = x.astype(F32)
    z_f = z.astype(F32)
    x_base = quotient(jnp.full((1, 1), 187.0) * x_f, 4)
    z_row = quotient(187.0 * (NZ * x_f + z_to), 48) - x_base + (z_chunk - 5.0 * z_tile)
    z_pick = (iota((XROWS, 3 * TROWS), 1) == z_tile * TROWS + z_row) & (z_chunk < 15.0)
    z_pick = jnp.where(z_pick, 1.0, 0.0).astype(BF16)

    y_place = iota((NY * 16, 64), 0)
    y_to = quotient(y_place, 16)
    y_chunk = y_place - 16.0 * y_to
    y_half = jnp.where(y_chunk < 6.0, y_chunk, y_chunk - 6.0)
    y_second = jnp.where(y_half < 3.0, 0.0, 1.0)
    y_tile = y_half - 3.0 * y_second
    z_base = quotient(jnp.full((1, 1), 187.0) * seq_f, 48)
    y_row = quotient(187.0 * (NY * seq_f + y_to), 384) - z_base + y_second
    y_at = jnp.where(
        y_chunk < 6.0, 16.0 * y_tile + 2.0 * y_to + y_second, 48.0 + 5.0 * y_tile + y_row
    )
    y_there = (y_chunk < 6.0) | ((y_chunk < 12.0) & (y_row < 5.0))
    y_pick = (iota((NY * 16, 64), 1) == y_at) & y_there
    y_pick = jnp.where(y_pick, 1.0, 0.0).astype(BF16)

    for copy in rows_copies:
        copy.wait_recv()
    from_donor = jnp.concatenate([rows_in[h, 0:CAP, :] for h in range(HOPS)], axis=0)
    from_acceptor = jnp.concatenate(
        [rows_in[HOPS - 1 - h, CAP : 2 * CAP, :] for h in range(HOPS)], axis=0
    )
    other = jnp.concatenate([from_donor, dot(unchosen, from_acceptor).astype(BF16)], axis=0)
    other_f = other.astype(F32)
    pair = (own_rows.astype(F32) * other_f).astype(BF16)
    raw = dot(pair, scale[...], 1, 1) * inv_root
    small = jnp.exp(-jnp.abs(raw))
    sigmoid = jnp.where(raw >= 0.0, 1.0, small) / (1.0 + small)
    all_cot = jnp.concatenate([in_cot, cot[...].astype(F32) * live_col], axis=0)
    slope = (all_cot * sigmoid).astype(BF16)
    terms = dot(slope, scale[...]) * other_f * inv_root
    junction = dot(spread, terms.astype(BF16))
    for k in range(2):
        cols = slice(k * HALF, (k + 1) * HALF)
        total = fcot[:, cols].astype(F32) + junction[:, cols]
        pre[k] = (total * act[:, cols]).astype(BF16)
    pre_copy = remote(pre.at[1 - core], pre_in, S_PRE, partner)
    pre_copy.start()

    slope_s = dot(pre[0], mix[:, :HALF], 1, 1) + dot(pre[1], mix[:, HALF:], 1, 1)
    slope_s = slope_s.astype(BF16)
    spad[8 : 8 + ROWS, :] = slope_s.astype(F32)
    edge_out[0] = slope_s[ROWS - 16 :]
    edge_out[1] = slope_s[:16]
    edge_right = remote(edge_out.at[0], edge_in.at[0], S_SLOPE, along_seq(1))
    edge_left = remote(edge_out.at[1], edge_in.at[1], S_SLOPE + 1, along_seq(-1))
    edge_right.start()
    edge_left.start()

    tissue = dot(slope[BUCKET:].T, pair[BUCKET:]) * inv_root
    depth = []
    for k in range(3):
        part = jnp.zeros((1, CH), F32)
        for at in range(0, ROWS, step_rows):
            part = part + jnp.sum(
                fpad[at + 7 + k : at + 7 + k + step_rows, :]
                * spad[at + 8 : at + 8 + step_rows, :],
                axis=0,
                keepdims=True,
            )
        depth.append(part * grad_scale)
    depth = jnp.concatenate(depth + [jnp.zeros((5, CH), F32)], axis=0)
    for k in range(2):
        cols = slice(k * HALF, (k + 1) * HALF)
        head[k, 0:TRACKS, :] = tissue[:, cols]
        head[k, TRACKS:HEAD_PAD, :] = depth[:, cols]
        head_cast[k] = head[k].astype(BF16)
    head_copy = remote(head_cast.at[1 - core], head_in, S_HEAD, partner)
    head_copy.start()

    smooth_copy.wait_recv()
    pre_copy.wait_recv()
    pre_own = pre[core]
    pre_other = pre_in[...]
    xm_copies = {}
    for step in (2, 1, 3):
        to = lax.rem(x + step, NX)
        block = dot(smooth[to], pre_own) + dot(smooth_in[to], pre_other)
        xm_out[step - 1] = block.astype(BF16)
        xm_copies[step] = remote(
            xm_out.at[step - 1], xm_in.at[step - 1], S_XM + step - 1, along_x(step)
        )
        xm_copies[step].start()
    xm_own[...] = dot(smooth[x], pre_own) + dot(smooth_in[x], pre_other)

    head_copy.wait_recv()
    head[core] = head[core] + head_in[...].astype(F32)
    for k in range(NX):
        base = (187 * k) // 4
        xt_out[k] = head[core, base : base + TROWS, :].astype(BF16)
    xt_copies = {}
    for step in (2, 1, 3):
        to = lax.rem(x + step, NX)
        xt_copies[step] = remote(
            xt_out.at[to], xt_in.at[step - 1], S_XT + step - 1, along_x(step)
        )
        xt_copies[step].start()

    edge_right.wait_recv()
    edge_left.wait_recv()
    spad[0:8, :] = edge_in[0].astype(F32)[8:16] * inner_low
    spad[8 + ROWS : 16 + ROWS, :] = edge_in[1].astype(F32)[0:8] * inner_high
    for at in range(0, ROWS, step_rows):
        total = spad[at + 9 : at + 9 + step_rows, :] * tap[0]
        total = total + spad[at + 8 : at + 8 + step_rows, :] * tap[1]
        total = total + spad[at + 7 : at + 7 + step_rows, :] * tap[2]
        grad_out[at : at + step_rows, :] = total.astype(BF16)
    raw_d = raw[BUCKET:]
    softplus = jnp.maximum(raw_d, 0.0) + jnp.log1p(small[BUCKET:])
    scores_out[...] = softplus * live_col

    for step in range(1, NX):
        xm_copies[step].wait_recv()
    total = xm_own[...]
    for step in range(1, NX):
        total = total + xm_in[step - 1].astype(F32)
    for step in range(1, NX):
        xt_copies[step].wait_recv()
    tail = xt_out[x].astype(F32)
    for step in range(1, NX):
        tail = tail + xt_in[step - 1].astype(F32)
    tail = tail.astype(BF16)
    stacked = jnp.concatenate([tail[:, k * 128 : (k + 1) * 128] for k in range(3)], axis=0)
    chunks = dot(z_pick, stacked).astype(BF16)
    joined = jnp.concatenate([total.astype(BF16), chunks], axis=1)
    for k in range(NZ):
        z_out[k] = joined[k * ZROWS : (k + 1) * ZROWS]

    def z_copy(step):
        return remote(
            z_out.at[lax.rem(z + step, NZ)], z_in.at[step - 1], S_Z + step - 1, along_z(step)
        )

    @pl.loop(1, NZ)
    def _(step):
        z_copy(step).start()

    def z_add(step, total):
        z_copy(step).wait_recv()
        return total + z_in[step - 1].astype(F32)

    total = lax.fori_loop(1, NZ, z_add, z_out[z].astype(F32)).astype(BF16)
    stacked = jnp.concatenate([total[:, k * 128 : (k + 1) * 128] for k in range(4)], axis=0)
    chunks = dot(y_pick, stacked).astype(BF16)
    for k in range(NY):
        y_out[k] = chunks[k * 16 : (k + 1) * 16]

    def y_copy(step):
        return remote(
            y_out.at[lax.rem(y + step, NY)], y_in.at[step - 1], S_Y + step - 1, along_y(step)
        )

    @pl.loop(1, NY)
    def _(step):
        y_copy(step).start()

    def y_add(step, total):
        y_copy(step).wait_recv()
        return total + y_in[step - 1].astype(F32)

    total = lax.fori_loop(1, NY, y_add, y_out[y].astype(F32))

    end_out[...] = total
    end_copy = remote(end_out, end_in, S_END, partner)
    end_copy.start()
    end_copy.wait_recv()
    far = end_in[...]
    first = core == 0
    low = jnp.where(first, total, far)
    high = jnp.where(first, far, total)

    def strip(source, base):
        return [source[base + k : base + k + 1, :] for k in range(3)]

    row = [
        jnp.concatenate(strip(low, 3 * k) + strip(high, 3 * k), axis=1) for k in range(2)
    ]
    conv_out[...] = jnp.where(first, row[0], row[1]) * grad_scale
    line = jnp.concatenate(
        strip(low, 6) + strip(high, 6) + strip(low, 9) + strip(high, 9), axis=1
    )
    number = seq * NY + y
    begin = number * (2 * SHARE) - lax.div(number * (2 * SHARE), CH) * CH + core * SHARE
    line = jnp.broadcast_to(line, (8, 2 * CH))
    line = pltpu.roll(line, lax.rem(2 * CH - begin, 2 * CH), 1)
    head_out[...] = line[0:1, :SHARE]

    for copy in code_copies + rows_copies:
        copy.wait_send()
    for copy in (feat_right, feat_left, edge_right, edge_left):
        copy.wait_send()
    for copy in (smooth_copy, pre_copy, head_copy, end_copy):
        copy.wait_send()
    for step in range(1, NX):
        xm_copies[step].wait_send()
        xt_copies[step].wait_send()

    @pl.loop(1, NZ)
    def _(step):
        z_copy(step).wait_send()

    @pl.loop(1, NY)
    def _(step):
        y_copy(step).wait_send()


def on_device(
    features,
    feature_cot,
    depth_weight,
    mix_weight,
    tissue_scale,
    donor_site,
    acceptor_hop,
    acceptor_site,
    live_count,
    score_cot,
):
    vmem = pl.BlockSpec(memory_space=pltpu.VMEM)

    def room(*shape, dtype=BF16):
        return pltpu.VMEM(shape, dtype)

    scores, grad, conv, head = pl.pallas_call(
        body,
        out_shape=(
            jax.ShapeDtypeStruct((SLOTS, TRACKS), F32),
            jax.ShapeDtypeStruct((ROWS, CH), BF16),
            jax.ShapeDtypeStruct((1, CH), F32),
            jax.ShapeDtypeStruct((1, SHARE), F32),
        ),
        in_specs=[vmem] * 10,
        out_specs=(vmem,) * 4,
        scratch_shapes=[
            room(HOPS, CAP, 384),
            room(HOPS, CAP, 384),
            room(HOPS, 2 * CAP, CH),
            room(HOPS, 2 * CAP, CH),
            room(2, 16, CH),
            room(2, 16, CH),
            room(2, 16, CH),
            room(ROWS + 16, CH, dtype=F32),
            room(ROWS + 16, CH, dtype=F32),
            room(ROWS, CH, dtype=F32),
            room(ROWS, CH),
            room(NX, XROWS, ROWS),
            room(NX, XROWS, ROWS),
            room(2, ROWS, HALF),
            room(ROWS, HALF),
            room(2, HEAD_PAD, HALF, dtype=F32),
            room(2, HEAD_PAD, HALF),
            room(HEAD_PAD, HALF),
            room(NX - 1, XROWS, HALF),
            room(XROWS, HALF, dtype=F32),
            room(NX - 1, XROWS, HALF),
            room(NX, TROWS, HALF),
            room(NX - 1, TROWS, HALF),
            room(NZ, ZROWS, 512),
            room(NZ - 1, ZROWS, 512),
            room(NY, 16, 128),
            room(NY - 1, 16, 128),
            room(16, 128, dtype=F32),
            room(16, 128, dtype=F32),
            pltpu.SemaphoreType.DMA((S_ALL,)),
            pltpu.SemaphoreType.DMA((S_ALL,)),
        ],
        compiler_params=pltpu.CompilerParams(
            collective_id=0, has_side_effects=True, vmem_limit_bytes=40 * 1024 * 1024
        ),
    )(
        features[0],
        feature_cot[0],
        depth_weight,
        mix_weight,
        tissue_scale,
        donor_site,
        acceptor_hop.reshape(1, SLOTS),
        acceptor_site,
        live_count,
        score_cot[0].T,
    )
    return scores.T[None], grad[None], conv.reshape(CH), head.reshape(SHARE)


def solution(mesh):
    placed = (
        P("dp", "seq", None),
        P("dp", "seq", None),
        P(),
        P(),
        P(),
        P("dp", "seq"),
        P("dp", "seq", None),
        P("dp", "seq"),
        P("dp", "seq"),
        P("dp", None, "seq"),
    )
    return jax.shard_map(
        on_device,
        mesh=mesh,
        in_specs=placed,
        out_specs=(P("dp", None, "seq"), P("dp", "seq", None), P(("seq", "dp")), P(("seq", "dp"))),
        check_vma=False,
    )
```

time: 627 us -> 71.5 us (0.11)
  waiting for transfers between devices: 498 us -> 0 us
  starting transfers between devices: 79.5 us -> 0 us
  Pallas kernels: 0 us -> 59.6 us
  other arithmetic: 16.5 us -> 0.61 us
  between operations: 15.5 us -> 1.31 us
    unnamed x2 -> x0, waiting for transfers between devices: 485 us -> none
    ppermute x24 -> x0, starting transfers between devices: 79.4 us -> none  [the longest x20 67.1 us: from_behind(): return lax.ppermute(block, axis, route)]
    pallas_call x0 -> x1, Pallas kernels: none -> 59.6 us  [on_device(): pl.pallas_call(body, out_shape=(jax.ShapeDtypeStruct((SLOTS, TRACKS), F32...]
    ppermute x24 -> x0, waiting for transfers between devices: 13.3 us -> none  [the longest x20 11.1 us: from_behind(): return lax.ppermute(block, axis, route)]
    unnamed x44 -> x21, local copies, waits for them, and re-layouts: 2.82 us -> 9.56 us
  transfers between devices with their start and end apart: 25 -> 0, of which waited for: 7 -> 0; matrix products, arithmetic and copies ran while one was open for 3% -> 0% of each run, Pallas kernels for 0% -> 0%
where the time goes in v1:
time: 71.5 us; the launch traced here: 71 us
  Pallas kernels  59.6 us (83%)
  local copies, waits for them, and re-layouts  9.56 us (13%)
  between operations  1.31 us (2%)
    pallas_call x1, Pallas kernels, on_device(): pl.pallas_call(body, out_shape=(jax.ShapeDtypeStruct((SLOTS, TRACKS), F32...  59.6 us
    unnamed x21, local copies, waits for them, and re-layouts  9.56 us

profile of v1, /device:TPU:1, one launch (start us, length us, event | category | flops | bytes accessed | tf_op | source)
XLA Modules:
  0.0 71.0 jit_solution(4855818574725853166)
XLA Ops:
  1.3 0.0 copy-start
  1.3 1.3 %copy-done = bf16[768,768]{1,0:T(8,128)(2,1)S(1)} copy-done((bf16[768,768]{1,0:T(8,128)(2,1)S(1)}, bf16[768,768]{1,0:T(8,128)(2,1)}, u32[]{:S(2)}) %copy-start) | copy-done | bytes 1179672
  2.6 0.0 copy-start.1
  2.6 1.0 %copy-done.1 = bf16[1,256,768]{2,1,0:T(8,128)(2,1)S(1)} copy-done((bf16[1,256,768]{2,1,0:T(8,128)(2,1)S(1)}, bf16[1,256,768]{2,1,0:T(8,128)(2,1)}, u32[]{:S(2)}) %copy-start.1) | copy-done | bytes 393240
  3.5 0.0 copy-start.2
  3.6 1.0 %copy-done.2 = bf16[1,256,768]{2,1,0:T(8,128)(2,1)S(1)} copy-done((bf16[1,256,768]{2,1,0:T(8,128)(2,1)S(1)}, bf16[1,256,768]{2,1,0:T(8,128)(2,1)}, u32[]{:S(2)}) %copy-start.2) | copy-done | bytes 393240
  4.5 0.0 copy-start.3
  4.5 1.0 %copy-done.3 = bf16[184,768]{1,0:T(8,128)(2,1)S(1)} copy-done((bf16[184,768]{1,0:T(8,128)(2,1)S(1)}, bf16[184,768]{1,0:T(8,128)(2,1)}, u32[]{:S(2)}) %copy-start.3) | copy-done | bytes 282648
  5.5 0.0 copy-start.4
  5.5 0.8 %copy-done.4 = bf16[1,184,64]{1,2,0:T(8,128)(2,1)S(1)} copy-done((bf16[1,184,64]{1,2,0:T(8,128)(2,1)S(1)}, bf16[1,184,64]{1,2,0:T(8,128)(2,1)}, u32[]{:S(2)}) %copy-start.4) | copy-done | bytes 23576
  6.3 0.0 copy-start.5
  6.3 0.7 copy-done.5
  7.0 0.0 copy-start.6
  7.0 0.7 copy-done.6
  7.6 0.0 copy-start.7
  7.6 0.7 copy-done.7
  8.3 0.0 copy-start.8
  8.3 0.7 copy-done.8
  8.9 59.6 %shard_map.129 = (f32[64,184]{1,0:T(8,128)S(1)}, bf16[256,768]{1,0:T(8,128)(2,1)S(1)}, f32[1,768]{1,0:T(1,128)S(1)}, f32[1,187]{1,0:T(1,128)S(1)}) custom-call(bf16[256,768]{1,0:T(8,128)(2,1)S(1)} %bitcast.11, bf16[256,768]{1,0:T(8,128)(2,1)S(1)} %bitcast.12, bf16[3,768]{1,0:T(4,128)(2,1)S(1)} %copy-done.5, bf16[768,768]{1,0:T(8,128)(2,1)S(1)} %copy-done, ...), custom_call_target="tpu_custom_call" | custom-call | tf_op jit(solution)/shard_map/pallas_call | solution.py:506
  68.5 0.6 reduce
  69.1 0.6 copy.18
  69.7 0.7 %copy.19 = bf16[1,256,768]{2,1,0:T(8,128)(2,1)} copy(bf16[1,256,768]{2,1,0:T(8,128)(2,1)S(1)} %bitcast.13) | data formatting | bytes 786432
  70.5 0.6 copy.20
Async XLA Ops:
  1.3 1.3 %copy-start = (bf16[768,768]{1,0:T(8,128)(2,1)S(1)}, bf16[768,768]{1,0:T(8,128)(2,1)}, u32[]{:S(2)}) copy-start(bf16[768,768]{1,0:T(8,128)(2,1)} %mix.1) | copy-start | bytes 3538948
  2.6 1.0 %copy-start.1 = (bf16[1,256,768]{2,1,0:T(8,128)(2,1)S(1)}, bf16[1,256,768]{2,1,0:T(8,128)(2,1)}, u32[]{:S(2)}) copy-start(bf16[1,256,768]{2,1,0:T(8,128)(2,1)} %param.10) | copy-start | bytes 1179652
  3.5 1.0 %copy-start.2 = (bf16[1,256,768]{2,1,0:T(8,128)(2,1)S(1)}, bf16[1,256,768]{2,1,0:T(8,128)(2,1)}, u32[]{:S(2)}) copy-start(bf16[1,256,768]{2,1,0:T(8,128)(2,1)} %param.11) | copy-start | bytes 1179652
  4.5 1.0 %copy-start.3 = (bf16[184,768]{1,0:T(8,128)(2,1)S(1)}, bf16[184,768]{1,0:T(8,128)(2,1)}, u32[]{:S(2)}) copy-start(bf16[184,768]{1,0:T(8,128)(2,1)} %scale.1) | copy-start | bytes 847876
  5.5 0.8 %copy-start.4 = (bf16[1,184,64]{1,2,0:T(8,128)(2,1)S(1)}, bf16[1,184,64]{1,2,0:T(8,128)(2,1)}, u32[]{:S(2)}) copy-start(bf16[1,184,64]{1,2,0:T(8,128)(2,1)} %param.19) | copy-start | bytes 70660
  6.3 0.7 copy-start.5
  7.0 0.7 copy-start.6
  7.6 0.7 copy-start.7
  8.3 0.7 copy-start.8

commit v2 on v1

--- a/solution.py
+++ b/solution.py
@@ -16,6 +16,7 @@
 CAP = 16
 NX, NZ, NY, NC = 4, 12, 8, 2
 SHARDS = NX * NZ
+DP = NY * NC
 ROWS = 256
 CH = 768
 HALF = CH // 2
@@ -30,9 +31,17 @@
 SHARE = HEAD * CH // (SHARDS * NY * NC)
 
 S_CODE, S_ROWS, S_FEAT, S_SLOPE = 0, 5, 10, 12
-S_SMOOTH, S_PRE, S_HEAD, S_END = 14, 15, 16, 17
-S_XM, S_XT, S_Z, S_Y = 18, 21, 24, 35
-S_ALL = 42
+S_SMOOTH, S_PRE, S_HEAD = 14, 15, 16
+S_XT, S_Z, S_Y = 20, 23, 34
+S_T, S_TAPS, S_TAPS_X, S_TAPS_Z = 49, 60, 61, 64
+S_XM = 75
+S_ALL = 84
+
+X_FAR, X_NEAR = (2, 1, 3), (1, 3, 2)
+Z_FAR = (6, 5, 7, 4, 8, 3, 9, 2, 10, 1, 11)
+PIECES = ((6, 5, 7, 4), (8, 3, 9, 2), (10, 1, 11, 0))
+PROWS = ZROWS * len(PIECES[0])
+D_FAR = (8, 7, 9, 6, 10, 5, 11, 4, 12, 3, 13, 2, 14, 1, 15)
 
 
 def dot(a, b, left=1, right=0):
@@ -49,7 +58,28 @@
     return jnp.floor((value + 0.5) * (1.0 / divisor))
 
 
-def body(
+def body(*refs):
+    operands, targets, refs = refs[:10], refs[10:14], refs[14:]
+    local, refs = refs[-1], refs[:-1]
+    held, refs = refs[-10:], refs[:-10]
+    loads = [
+        pltpu.make_async_copy(src, dst, local.at[k])
+        for k, (src, dst) in enumerate(zip(operands, held))
+    ]
+    for k in (0, 6, 8, 5, 7, 9, 2, 3, 4, 1):
+        loads[k].start()
+    stores = [
+        pltpu.make_async_copy(src, dst, local.at[10 + k])
+        for k, (src, dst) in enumerate(zip(refs[:4], targets))
+    ]
+    steps(loads, stores, *held, *refs)
+    for copy in stores:
+        copy.wait()
+
+
+def steps(
+    loads,
+    stores,
     feat,
     fcot,
     taps,
@@ -88,11 +118,20 @@
     xt_out,
     xt_in,
     z_out,
+    z_own,
     z_in,
-    y_out,
-    y_in,
-    end_out,
-    end_in,
+    t_out,
+    t_in,
+    tail_sum,
+    taps_part,
+    taps_cast,
+    taps_in,
+    taps_sum,
+    taps_out,
+    taps_x,
+    taps_z,
+    d_out,
+    d_in,
     send,
     recv,
 ):
@@ -112,8 +151,8 @@
     def along_z(step):
         return {"seq": x * NZ + lax.rem(z + step, NZ), "dp": dp}
 
-    def along_y(step):
-        return {"seq": seq, "dp": lax.rem(y + step, NY) * NC + core}
+    def along_dp(step):
+        return {"seq": seq, "dp": lax.rem(dp + step, DP)}
 
     partner = {"seq": seq, "dp": y * NC + 1 - core}
 
@@ -127,6 +166,16 @@
             device_id_type=MESH,
         )
 
+    leaving = []
+
+    def start(copy):
+        copy.start()
+        leaving.append(copy)
+
+    def done():
+        for copy in leaving:
+            copy.wait_send()
+
     barrier = pltpu.get_barrier_semaphore()
 
     def greet(device):
@@ -134,7 +183,6 @@
 
     for step in (-2, -1, 1, 2):
         greet(along_seq(step))
-    greet(partner)
     for step in range(1, NX):
         greet(along_x(step))
 
@@ -142,9 +190,20 @@
     def _(step):
         greet(along_z(step))
 
-    @pl.loop(1, NY)
+    @pl.loop(1, DP)
     def _(step):
-        greet(along_y(step))
+        greet(along_dp(step))
+
+    loads[0].wait()
+    pl.semaphore_wait(barrier, 4 + (NX - 1) + (NZ - 1) + (DP - 1))
+
+    feat_right = remote(feat.at[pl.ds(ROWS - 16, 16)], halo_in.at[0], S_FEAT, along_seq(1))
+    feat_left = remote(feat.at[pl.ds(0, 16)], halo_in.at[1], S_FEAT + 1, along_seq(-1))
+    start(feat_right)
+    start(feat_left)
+
+    for k in (5, 6, 7, 8, 9):
+        loads[k].wait()
 
     hop_row = hop[...].astype(F32)
     seq_f = seq.astype(F32)
@@ -191,19 +250,15 @@
 
     fpad[8 : 8 + ROWS, :] = feat[...].astype(F32)
 
-    pl.semaphore_wait(barrier, 4 + 1 + (NX - 1) + (NZ - 1) + (NY - 1))
-
     others = [h for h in range(HOPS) if h != REACH]
-    feat_right = remote(feat.at[pl.ds(ROWS - 16, 16)], halo_in.at[0], S_FEAT, along_seq(1))
-    feat_left = remote(feat.at[pl.ds(0, 16)], halo_in.at[1], S_FEAT + 1, along_seq(-1))
-    feat_right.start()
-    feat_left.start()
     code_copies = [
         remote(code_out.at[h], code_in.at[h], S_CODE + h, along_seq(h - REACH)) for h in others
     ]
     for copy in code_copies:
-        copy.start()
-
+        start(copy)
+
+    for k in (1, 2, 3, 4):
+        loads[k].wait()
     feat_right.wait_recv()
     feat_left.wait_recv()
     inner_low = jnp.where(seq > 0, 1.0, 0.0)
@@ -221,9 +276,11 @@
     act[...] = dot(smoothed, mix[...])
     turned = smoothed.T
     for k in range(NX):
-        smooth[k] = turned[k * XROWS : (k + 1) * XROWS]
+        for j in range(NZ):
+            at = k * XROWS + j * ZROWS
+            smooth[k, j] = turned[at : at + ZROWS]
     smooth_copy = remote(smooth, smooth_in, S_SMOOTH, partner)
-    smooth_copy.start()
+    start(smooth_copy)
 
     root = math.sqrt(2.0 / math.pi)
 
@@ -266,7 +323,7 @@
         remote(rows_out.at[h], rows_in.at[h], S_ROWS + h, along_seq(h - REACH)) for h in others
     ]
     for copy in rows_copies:
-        copy.start()
+        start(copy)
 
     spread = hot[:both].T
 
@@ -281,20 +338,21 @@
     z_pick = (iota((XROWS, 3 * TROWS), 1) == z_tile * TROWS + z_row) & (z_chunk < 15.0)
     z_pick = jnp.where(z_pick, 1.0, 0.0).astype(BF16)
 
-    y_place = iota((NY * 16, 64), 0)
-    y_to = quotient(y_place, 16)
-    y_chunk = y_place - 16.0 * y_to
-    y_half = jnp.where(y_chunk < 6.0, y_chunk, y_chunk - 6.0)
-    y_second = jnp.where(y_half < 3.0, 0.0, 1.0)
-    y_tile = y_half - 3.0 * y_second
+    d_place = iota((DP * 16, 64), 0)
+    d_to = quotient(d_place, 16)
+    d_chip = quotient(d_to, NC)
+    d_chunk = d_place - 16.0 * d_to
+    d_half = d_chunk - 3.0
+    d_second = jnp.where(d_half < 3.0, 0.0, 1.0)
+    d_tile = d_half - 3.0 * d_second
     z_base = quotient(jnp.full((1, 1), 187.0) * seq_f, 48)
-    y_row = quotient(187.0 * (NY * seq_f + y_to), 384) - z_base + y_second
-    y_at = jnp.where(
-        y_chunk < 6.0, 16.0 * y_tile + 2.0 * y_to + y_second, 48.0 + 5.0 * y_tile + y_row
-    )
-    y_there = (y_chunk < 6.0) | ((y_chunk < 12.0) & (y_row < 5.0))
-    y_pick = (iota((NY * 16, 64), 1) == y_at) & y_there
-    y_pick = jnp.where(y_pick, 1.0, 0.0).astype(BF16)
+    d_row = quotient(187.0 * (NY * seq_f + d_chip), 384) - z_base + d_second
+    d_at = jnp.where(
+        d_chunk < 3.0, 16.0 * d_chunk + d_to, 48.0 + 5.0 * d_tile + d_row
+    )
+    d_there = (d_chunk < 3.0) | ((d_chunk < 9.0) & (d_row < 5.0))
+    d_pick = (iota((DP * 16, 64), 1) == d_at) & d_there
+    d_pick = jnp.where(d_pick, 1.0, 0.0).astype(BF16)
 
     for copy in rows_copies:
         copy.wait_recv()
@@ -310,6 +368,13 @@
     sigmoid = jnp.where(raw >= 0.0, 1.0, small) / (1.0 + small)
     all_cot = jnp.concatenate([in_cot, cot[...].astype(F32) * live_col], axis=0)
     slope = (all_cot * sigmoid).astype(BF16)
+    tissue = dot(slope[BUCKET:].T, pair[BUCKET:]) * inv_root
+    tissue = jnp.concatenate([tissue, jnp.zeros((HEAD_PAD - TRACKS, CH), F32)], axis=0)
+    for k in range(2):
+        head[k] = tissue[:, k * HALF : (k + 1) * HALF]
+        head_cast[k] = head[k].astype(BF16)
+    head_copy = remote(head_cast.at[1 - core], head_in, S_HEAD, partner)
+    start(head_copy)
     terms = dot(slope, scale[...]) * other_f * inv_root
     junction = dot(spread, terms.astype(BF16))
     for k in range(2):
@@ -317,7 +382,46 @@
         total = fcot[:, cols].astype(F32) + junction[:, cols]
         pre[k] = (total * act[:, cols]).astype(BF16)
     pre_copy = remote(pre.at[1 - core], pre_in, S_PRE, partner)
-    pre_copy.start()
+    start(pre_copy)
+
+    head_copy.wait_recv()
+    head[core] = head[core] + head_in[...].astype(F32)
+    for k in range(NX):
+        base = (187 * k) // 4
+        xt_out[k] = head[core, base : base + TROWS, :].astype(BF16)
+    xt_copies = {}
+    for step in X_FAR:
+        to = lax.rem(x + step, NX)
+        xt_copies[step] = remote(
+            xt_out.at[to], xt_in.at[step - 1], S_XT + step - 1, along_x(step)
+        )
+        start(xt_copies[step])
+
+    smooth_copy.wait_recv()
+    pre_copy.wait_recv()
+    pre_own = pre[core]
+    pre_other = pre_in[...]
+    xm_copies = {}
+    for n, piece in enumerate(PIECES):
+        order = [lax.rem(x + step, NX) for step in (*X_FAR, 0)]
+        parts = [
+            jnp.concatenate(
+                [source[to, lax.rem(z + step, NZ)] for to in order for step in piece], axis=0
+            )
+            for source in (smooth, smooth_in)
+        ]
+        block = dot(parts[0], pre_own) + dot(parts[1], pre_other)
+        for k, step in enumerate(X_FAR):
+            xm_out[n, step - 1] = block[k * PROWS : (k + 1) * PROWS].astype(BF16)
+            copy = remote(
+                xm_out.at[n, step - 1],
+                xm_in.at[n, step - 1],
+                S_XM + n * (NX - 1) + step - 1,
+                along_x(step),
+            )
+            start(copy)
+            xm_copies[n, step] = copy
+        xm_own[n] = block[(NX - 1) * PROWS :]
 
     slope_s = dot(pre[0], mix[:, :HALF], 1, 1) + dot(pre[1], mix[:, HALF:], 1, 1)
     slope_s = slope_s.astype(BF16)
@@ -326,10 +430,49 @@
     edge_out[1] = slope_s[:16]
     edge_right = remote(edge_out.at[0], edge_in.at[0], S_SLOPE, along_seq(1))
     edge_left = remote(edge_out.at[1], edge_in.at[1], S_SLOPE + 1, along_seq(-1))
-    edge_right.start()
-    edge_left.start()
-
-    tissue = dot(slope[BUCKET:].T, pair[BUCKET:]) * inv_root
+    start(edge_right)
+    start(edge_left)
+
+    for step in X_NEAR:
+        xt_copies[step].wait_recv()
+    tail = xt_out[x].astype(F32)
+    for step in range(1, NX):
+        tail = tail + xt_in[step - 1].astype(F32)
+    tail = tail.astype(BF16)
+    stacked = jnp.concatenate([tail[:, k * 128 : (k + 1) * 128] for k in range(3)], axis=0)
+    chunks = dot(z_pick, stacked).astype(BF16)
+    for k in range(NZ):
+        t_out[k] = chunks[k * ZROWS : (k + 1) * ZROWS]
+
+    def t_copy(step):
+        return remote(
+            t_out.at[lax.rem(z + step, NZ)], t_in.at[step - 1], S_T + step - 1, along_z(step)
+        )
+
+    t_copies = {step: t_copy(step) for step in range(1, NZ)}
+    for step in Z_FAR:
+        start(t_copies[step])
+
+    z_copies = {}
+
+    def pass_on(n):
+        total = xm_own[n]
+        for step in X_NEAR:
+            xm_copies[n, step].wait_recv()
+            total = total + xm_in[n, step - 1].astype(F32)
+        for k, step in enumerate(PIECES[n]):
+            rows = total[k * ZROWS : (k + 1) * ZROWS]
+            if step == 0:
+                z_own[...] = rows
+                continue
+            z_out[step - 1] = rows.astype(BF16)
+            z_copies[step] = remote(
+                z_out.at[step - 1], z_in.at[step - 1], S_Z + step - 1, along_z(step)
+            )
+            start(z_copies[step])
+
+    pass_on(0)
+
     depth = []
     for k in range(3):
         part = jnp.zeros((1, CH), F32)
@@ -341,42 +484,63 @@
                 keepdims=True,
             )
         depth.append(part * grad_scale)
-    depth = jnp.concatenate(depth + [jnp.zeros((5, CH), F32)], axis=0)
     for k in range(2):
-        cols = slice(k * HALF, (k + 1) * HALF)
-        head[k, 0:TRACKS, :] = tissue[:, cols]
-        head[k, TRACKS:HEAD_PAD, :] = depth[:, cols]
-        head_cast[k] = head[k].astype(BF16)
-    head_copy = remote(head_cast.at[1 - core], head_in, S_HEAD, partner)
-    head_copy.start()
-
-    smooth_copy.wait_recv()
-    pre_copy.wait_recv()
-    pre_own = pre[core]
-    pre_other = pre_in[...]
-    xm_copies = {}
-    for step in (2, 1, 3):
-        to = lax.rem(x + step, NX)
-        block = dot(smooth[to], pre_own) + dot(smooth_in[to], pre_other)
-        xm_out[step - 1] = block.astype(BF16)
-        xm_copies[step] = remote(
-            xm_out.at[step - 1], xm_in.at[step - 1], S_XM + step - 1, along_x(step)
+        lines = [
+            depth[tap_at][:, k * HALF + tile * 128 : k * HALF + tile * 128 + 128]
+            for tile in range(3)
+            for tap_at in range(3)
+        ]
+        total = jnp.concatenate(lines + [jnp.zeros((16 - 9, 128), F32)], axis=0)
+        taps_part[k] = total
+        taps_cast[k] = total.astype(BF16)
+    taps_copy = remote(taps_cast.at[1 - core], taps_in, S_TAPS, partner)
+    start(taps_copy)
+
+    pass_on(1)
+
+    taps_copy.wait_recv()
+    taps_sum[...] = taps_part[core] + taps_in[...].astype(F32)
+    last_x, last_z = x == NX - 1, (x == NX - 1) & (z == NZ - 1)
+
+    def taps_to_x(source):
+        return remote(
+            taps_out,
+            taps_x.at[source],
+            S_TAPS_X + source,
+            {"seq": (NX - 1) * NZ + z, "dp": dp},
         )
-        xm_copies[step].start()
-    xm_own[...] = dot(smooth[x], pre_own) + dot(smooth_in[x], pre_other)
-
-    head_copy.wait_recv()
-    head[core] = head[core] + head_in[...].astype(F32)
-    for k in range(NX):
-        base = (187 * k) // 4
-        xt_out[k] = head[core, base : base + TROWS, :].astype(BF16)
-    xt_copies = {}
-    for step in (2, 1, 3):
-        to = lax.rem(x + step, NX)
-        xt_copies[step] = remote(
-            xt_out.at[to], xt_in.at[step - 1], S_XT + step - 1, along_x(step)
+
+    def taps_to_z(source):
+        return remote(
+            taps_out,
+            taps_z.at[source],
+            S_TAPS_Z + source,
+            {"seq": NX * NZ - 1, "dp": dp},
         )
-        xt_copies[step].start()
+
+    for source in range(NX - 1):
+
+        @pl.when(x == source)
+        def _():
+            taps_out[...] = taps_sum[...].astype(BF16)
+            taps_to_x(source).start()
+
+    pass_on(2)
+
+    @pl.when(last_x)
+    def _():
+        total = taps_sum[...]
+        for source in range(NX - 1):
+            taps_to_x(source).wait_recv()
+            total = total + taps_x[source].astype(F32)
+        taps_sum[...] = total
+        taps_out[...] = total.astype(BF16)
+
+    for source in range(NZ - 1):
+
+        @pl.when(last_x & (z == source))
+        def _():
+            taps_to_z(source).start()
 
     edge_right.wait_recv()
     edge_left.wait_recv()
@@ -390,100 +554,99 @@
     raw_d = raw[BUCKET:]
     softplus = jnp.maximum(raw_d, 0.0) + jnp.log1p(small[BUCKET:])
     scores_out[...] = softplus * live_col
-
-    for step in range(1, NX):
-        xm_copies[step].wait_recv()
-    total = xm_own[...]
-    for step in range(1, NX):
-        total = total + xm_in[step - 1].astype(F32)
-    for step in range(1, NX):
-        xt_copies[step].wait_recv()
-    tail = xt_out[x].astype(F32)
-    for step in range(1, NX):
-        tail = tail + xt_in[step - 1].astype(F32)
-    tail = tail.astype(BF16)
-    stacked = jnp.concatenate([tail[:, k * 128 : (k + 1) * 128] for k in range(3)], axis=0)
-    chunks = dot(z_pick, stacked).astype(BF16)
-    joined = jnp.concatenate([total.astype(BF16), chunks], axis=1)
-    for k in range(NZ):
-        z_out[k] = joined[k * ZROWS : (k + 1) * ZROWS]
-
-    def z_copy(step):
+    stores[0].start()
+    stores[1].start()
+
+    tail = t_out[z].astype(F32)
+    for step in Z_FAR[::-1]:
+        t_copies[step].wait_recv()
+        tail = tail + t_in[step - 1].astype(F32)
+    tail_sum[...] = tail
+
+    @pl.when(last_z)
+    def _():
+        total = taps_sum[...]
+        for source in range(NZ - 1):
+            taps_to_z(source).wait_recv()
+            total = total + taps_z[source].astype(F32)
+        for tile in range(3):
+            at = 5 * tile + 1
+            tail_sum[at : at + 3, :] = tail_sum[at : at + 3, :] + total[3 * tile : 3 * tile + 3]
+
+    total = z_own[...]
+    for step in Z_FAR[::-1]:
+        z_copies[step].wait_recv()
+        total = total + z_in[step - 1].astype(F32)
+    total = jnp.concatenate([total, tail_sum[...]], axis=1).astype(BF16)
+    stacked = jnp.concatenate([total[:, k * 128 : (k + 1) * 128] for k in range(4)], axis=0)
+    chunks = dot(d_pick, stacked).astype(BF16)
+    for k in range(DP):
+        d_out[k] = chunks[k * 16 : (k + 1) * 16]
+
+    def d_copy(step):
         return remote(
-            z_out.at[lax.rem(z + step, NZ)], z_in.at[step - 1], S_Z + step - 1, along_z(step)
+            d_out.at[lax.rem(dp + step, DP)], d_in.at[step - 1], S_Y + step - 1, along_dp(step)
         )
 
-    @pl.loop(1, NZ)
-    def _(step):
-        z_copy(step).start()
-
-    def z_add(step, total):
-        z_copy(step).wait_recv()
-        return total + z_in[step - 1].astype(F32)
-
-    total = lax.fori_loop(1, NZ, z_add, z_out[z].astype(F32)).astype(BF16)
-    stacked = jnp.concatenate([total[:, k * 128 : (k + 1) * 128] for k in range(4)], axis=0)
-    chunks = dot(y_pick, stacked).astype(BF16)
-    for k in range(NY):
-        y_out[k] = chunks[k * 16 : (k + 1) * 16]
-
-    def y_copy(step):
-        return remote(
-            y_out.at[lax.rem(y + step, NY)], y_in.at[step - 1], S_Y + step - 1, along_y(step)
-        )
-
-    @pl.loop(1, NY)
-    def _(step):
-        y_copy(step).start()
-
-    def y_add(step, total):
-        y_copy(step).wait_recv()
-        return total + y_in[step - 1].astype(F32)
-
-    total = lax.fori_loop(1, NY, y_add, y_out[y].astype(F32))
-
-    end_out[...] = total
-    end_copy = remote(end_out, end_in, S_END, partner)
-    end_copy.start()
-    end_copy.wait_recv()
-    far = end_in[...]
+    d_copies = {step: d_copy(step) for step in range(1, DP)}
+    for step in D_FAR:
+        start(d_copies[step])
+    sums = [d_out[dp].astype(F32), jnp.zeros((16, 128), F32)]
+    for step in D_FAR[::-1]:
+        d_copies[step].wait_recv()
+        sums[step % 2] = sums[step % 2] + d_in[step - 1].astype(F32)
+
     first = core == 0
-    low = jnp.where(first, total, far)
-    high = jnp.where(first, far, total)
+    low = jnp.where(first, sums[0], sums[1])
+    high = jnp.where(first, sums[1], sums[0])
 
     def strip(source, base):
         return [source[base + k : base + k + 1, :] for k in range(3)]
 
-    row = [
-        jnp.concatenate(strip(low, 3 * k) + strip(high, 3 * k), axis=1) for k in range(2)
-    ]
-    conv_out[...] = jnp.where(first, row[0], row[1]) * grad_scale
+    conv_out[...] = jnp.concatenate(strip(low, 0) + strip(high, 0), axis=1) * grad_scale
+    stores[2].start()
     line = jnp.concatenate(
-        strip(low, 6) + strip(high, 6) + strip(low, 9) + strip(high, 9), axis=1
+        strip(low, 3) + strip(high, 3) + strip(low, 6) + strip(high, 6), axis=1
     )
     number = seq * NY + y
     begin = number * (2 * SHARE) - lax.div(number * (2 * SHARE), CH) * CH + core * SHARE
     line = jnp.broadcast_to(line, (8, 2 * CH))
     line = pltpu.roll(line, lax.rem(2 * CH - begin, 2 * CH), 1)
     head_out[...] = line[0:1, :SHARE]
-
-    for copy in code_copies + rows_copies:
-        copy.wait_send()
-    for copy in (feat_right, feat_left, edge_right, edge_left):
-        copy.wait_send()
-    for copy in (smooth_copy, pre_copy, head_copy, end_copy):
-        copy.wait_send()
-    for step in range(1, NX):
-        xm_copies[step].wait_send()
-        xt_copies[step].wait_send()
-
-    @pl.loop(1, NZ)
-    def _(step):
-        z_copy(step).wait_send()
-
-    @pl.loop(1, NY)
-    def _(step):
-        y_copy(step).wait_send()
+    stores[3].start()
+
+    done()
+    for source in range(NX - 1):
+
+        @pl.when(x == source)
+        def _():
+            taps_to_x(source).wait_send()
+
+    for source in range(NZ - 1):
+
+        @pl.when(last_x & (z == source))
+        def _():
+            taps_to_z(source).wait_send()
+
+
+def hand_over(*refs):
+    sources, targets, held, sems = refs[:4], refs[4:8], refs[8:12], refs[12]
+    loads = [
+        pltpu.make_async_copy(src, dst, sems.at[k])
+        for k, (src, dst) in enumerate(zip(sources, held))
+    ]
+    held = [held[0], held[1], held[2].at[0], held[3]]
+    stores = [
+        pltpu.make_async_copy(src, dst, sems.at[4 + k])
+        for k, (src, dst) in enumerate(zip(held, targets))
+    ]
+    for copy in loads:
+        copy.start()
+    for load, store in zip(loads, stores):
+        load.wait()
+        store.start()
+    for copy in stores:
+        copy.wait()
 
 
 def on_device(
@@ -499,21 +662,27 @@
     score_cot,
 ):
     vmem = pl.BlockSpec(memory_space=pltpu.VMEM)
+    hbm = pl.BlockSpec(memory_space=pltpu.HBM)
 
     def room(*shape, dtype=BF16):
         return pltpu.VMEM(shape, dtype)
 
-    scores, grad, conv, head = pl.pallas_call(
+    results = (
+        jax.ShapeDtypeStruct((SLOTS, TRACKS), F32),
+        jax.ShapeDtypeStruct((ROWS, CH), BF16),
+        jax.ShapeDtypeStruct((1, CH), F32),
+        jax.ShapeDtypeStruct((1, SHARE), F32),
+    )
+    made = pl.pallas_call(
         body,
-        out_shape=(
-            jax.ShapeDtypeStruct((SLOTS, TRACKS), F32),
-            jax.ShapeDtypeStruct((ROWS, CH), BF16),
-            jax.ShapeDtypeStruct((1, CH), F32),
-            jax.ShapeDtypeStruct((1, SHARE), F32),
-        ),
-        in_specs=[vmem] * 10,
-        out_specs=(vmem,) * 4,
+        out_shape=results,
+        in_specs=[hbm] * 10,
+        out_specs=(hbm,) * 4,
         scratch_shapes=[
+            room(SLOTS, TRACKS, dtype=F32),
+            room(ROWS, CH),
+            room(1, CH, dtype=F32),
+            room(1, SHARE, dtype=F32),
             room(HOPS, CAP, 384),
             room(HOPS, CAP, 384),
             room(HOPS, 2 * CAP, CH),
@@ -525,29 +694,49 @@
             room(ROWS + 16, CH, dtype=F32),
             room(ROWS, CH, dtype=F32),
             room(ROWS, CH),
-            room(NX, XROWS, ROWS),
-            room(NX, XROWS, ROWS),
+            room(NX, NZ, ZROWS, ROWS),
+            room(NX, NZ, ZROWS, ROWS),
             room(2, ROWS, HALF),
             room(ROWS, HALF),
             room(2, HEAD_PAD, HALF, dtype=F32),
             room(2, HEAD_PAD, HALF),
             room(HEAD_PAD, HALF),
-            room(NX - 1, XROWS, HALF),
-            room(XROWS, HALF, dtype=F32),
-            room(NX - 1, XROWS, HALF),
+            room(len(PIECES), NX - 1, PROWS, HALF),
+            room(len(PIECES), PROWS, HALF, dtype=F32),
+            room(len(PIECES), NX - 1, PROWS, HALF),
             room(NX, TROWS, HALF),
             room(NX - 1, TROWS, HALF),
-            room(NZ, ZROWS, 512),
-            room(NZ - 1, ZROWS, 512),
-            room(NY, 16, 128),
-            room(NY - 1, 16, 128),
+            room(NZ - 1, ZROWS, HALF),
+            room(ZROWS, HALF, dtype=F32),
+            room(NZ - 1, ZROWS, HALF),
+            room(NZ, ZROWS, 128),
+            room(NZ - 1, ZROWS, 128),
             room(16, 128, dtype=F32),
+            room(2, 16, 128, dtype=F32),
+            room(2, 16, 128),
+            room(16, 128),
             room(16, 128, dtype=F32),
+            room(16, 128),
+            room(NX - 1, 16, 128),
+            room(NZ - 1, 16, 128),
+            room(DP, 16, 128),
+            room(DP - 1, 16, 128),
             pltpu.SemaphoreType.DMA((S_ALL,)),
             pltpu.SemaphoreType.DMA((S_ALL,)),
+            room(ROWS, CH),
+            room(ROWS, CH),
+            room(3, CH),
+            room(CH, CH),
+            room(TRACKS, CH),
+            room(1, SLOTS, dtype=jnp.int32),
+            room(1, SLOTS, dtype=jnp.int32),
+            room(1, SLOTS, dtype=jnp.int32),
+            room(1, 1, dtype=jnp.int32),
+            room(SLOTS, TRACKS),
+            pltpu.SemaphoreType.DMA((14,)),
         ],
         compiler_params=pltpu.CompilerParams(
-            collective_id=0, has_side_effects=True, vmem_limit_bytes=40 * 1024 * 1024
+            collective_id=0, has_side_effects=True, vmem_limit_bytes=63 * 1024 * 1024
         ),
     )(
         features[0],
@@ -561,7 +750,21 @@
         live_count,
         score_cot[0].T,
     )
-    return scores.T[None], grad[None], conv.reshape(CH), head.reshape(SHARE)
+    scores, grad, conv, head = pl.pallas_call(
+        hand_over,
+        out_shape=results[:2] + (jax.ShapeDtypeStruct((CH,), F32), results[3]),
+        in_specs=[hbm] * 4,
+        out_specs=(hbm,) * 4,
+        scratch_shapes=[
+            room(SLOTS, TRACKS, dtype=F32),
+            room(ROWS, CH),
+            room(1, CH, dtype=F32),
+            room(1, SHARE, dtype=F32),
+            pltpu.SemaphoreType.DMA((8,)),
+        ],
+        compiler_params=pltpu.CompilerParams(vmem_limit_bytes=63 * 1024 * 1024),
+    )(*made)
+    return scores.T[None], grad[None], conv, head.reshape(SHARE)
 
 
 def solution(mesh):

time: 71.5 us -> 57.3 us (0.80)
  local copies, waits for them, and re-layouts: 9.56 us -> 0 us
  Pallas kernels: 59.6 us -> 55.8 us
    unnamed x21 -> x0, local copies, waits for them, and re-layouts: 9.56 us -> none
    pallas_call x1 -> x2, Pallas kernels: 59.6 us -> 55.8 us  [the longest x1 54 us: on_device(): pl.pallas_call(body, out_shape=results, in_specs=[hbm] * 10, out_specs=(h...]
where the time goes in v2:
time: 57.3 us; the launch traced here: 57.1 us
  Pallas kernels  55.8 us (97%)
  between operations  1.29 us (2%)
    pallas_call x1, Pallas kernels, on_device(): pl.pallas_call(body, out_shape=results, in_specs=[hbm] * 10, out_specs=(h...  54 us
    pallas_call x1, Pallas kernels, on_device(): pl.pallas_call(hand_over, out_shape=results[:2] + (jax.ShapeDtypeStruct((...  1.85 us

profile of v2, /device:TPU:1, one launch (start us, length us, event | category | flops | bytes accessed | tf_op | source)
XLA Modules:
  0.0 57.1 jit_solution(11871340001344239819)
XLA Ops:
  1.3 54.0 %shard_map.129 = (f32[64,184]{1,0:T(8,128)}, bf16[256,768]{1,0:T(8,128)(2,1)}, f32[1,768]{1,0:T(1,128)}, f32[1,187]{1,0:T(1,128)}) custom-call(bf16[256,768]{1,0:T(8,128)(2,1)} %bitcast.11, bf16[256,768]{1,0:T(8,128)(2,1)} %bitcast.12, bf16[3,768]{1,0:T(4,128)(2,1)} %refs_2_.1, bf16[768,768]{1,0:T(8,128)(2,1)} %refs_3_.1, bf16[184,768]{1,0:T(8,128)(2,1)} %refs_4_.1, ...), custom_call_target="tpu_custom_call" | custom-call | tf_op jit(solution)/shard_map/pallas_call | solution.py:676
  55.3 1.9 %shard_map.130 = (f32[64,184]{1,0:T(8,128)}, bf16[256,768]{1,0:T(8,128)(2,1)}, f32[768]{0:T(1024)}, f32[1,187]{1,0:T(1,128)}) custom-call(f32[64,184]{1,0:T(8,128)} %get-tuple-element.12.refs_0_, bf16[256,768]{1,0:T(8,128)(2,1)} %get-tuple-element.13.refs_1_, f32[1,768]{1,0:T(1,128)} %get-tuple-element.14.refs_2_, f32[1,187]{1,0:T(1,128)} %get-tuple-element.15.refs_3_), custom_call_target="tpu_custom_call" | custom-call | tf_op jit(solution)/shard_map/pallas_call | solution.py:753

commit v3 on v2

--- a/solution.py
+++ b/solution.py
@@ -52,6 +52,11 @@
 
 def iota(shape, dim):
     return lax.broadcasted_iota(jnp.int32, shape, dim).astype(F32)
+
+
+def wrapped(value, size):
+    value = jnp.where(value < 0, value + size, value)
+    return jnp.where(value >= size, value - size, value)
 
 
 def quotient(value, divisor):
@@ -104,6 +109,8 @@
     fpad,
     spad,
     act,
+    bend,
+    smooth_held,
     emb,
     smooth,
     smooth_in,
@@ -143,16 +150,16 @@
     grad_scale = 1.0 / math.sqrt(ROWS * SHARDS * NY * NC)
 
     def along_seq(step):
-        return {"seq": lax.rem(seq + SHARDS + step, SHARDS), "dp": dp}
+        return {"seq": wrapped(seq + step, SHARDS), "dp": dp}
 
     def along_x(step):
-        return {"seq": lax.rem(x + step, NX) * NZ + z, "dp": dp}
+        return {"seq": wrapped(x + step, NX) * NZ + z, "dp": dp}
 
     def along_z(step):
-        return {"seq": x * NZ + lax.rem(z + step, NZ), "dp": dp}
+        return {"seq": x * NZ + wrapped(z + step, NZ), "dp": dp}
 
     def along_dp(step):
-        return {"seq": seq, "dp": lax.rem(dp + step, DP)}
+        return {"seq": seq, "dp": wrapped(dp + step, DP)}
 
     partner = {"seq": seq, "dp": y * NC + 1 - core}
 
@@ -186,12 +193,9 @@
     for step in range(1, NX):
         greet(along_x(step))
 
-    @pl.loop(1, NZ)
-    def _(step):
+    for step in range(1, NZ):
         greet(along_z(step))
-
-    @pl.loop(1, DP)
-    def _(step):
+    for step in range(1, DP):
         greet(along_dp(step))
 
     loads[0].wait()
@@ -257,6 +261,33 @@
     for copy in code_copies:
         start(copy)
 
+    z_place = iota((XROWS, 3 * TROWS), 0)
+    z_to = quotient(z_place, ZROWS)
+    z_chunk = z_place - ZROWS * z_to
+    z_tile = quotient(z_chunk, 5)
+    x_f = x.astype(F32)
+    z_f = z.astype(F32)
+    x_base = quotient(jnp.full((1, 1), 187.0) * x_f, 4)
+    z_row = quotient(187.0 * (NZ * x_f + z_to), 48) - x_base + (z_chunk - 5.0 * z_tile)
+    z_pick = (iota((XROWS, 3 * TROWS), 1) == z_tile * TROWS + z_row) & (z_chunk < 15.0)
+    z_pick = jnp.where(z_pick, 1.0, 0.0).astype(BF16)
+
+    d_place = iota((DP * 16, 64), 0)
+    d_to = quotient(d_place, 16)
+    d_chip = quotient(d_to, NC)
+    d_chunk = d_place - 16.0 * d_to
+    d_half = d_chunk - 3.0
+    d_second = jnp.where(d_half < 3.0, 0.0, 1.0)
+    d_tile = d_half - 3.0 * d_second
+    z_base = quotient(jnp.full((1, 1), 187.0) * seq_f, 48)
+    d_row = quotient(187.0 * (NY * seq_f + d_chip), 384) - z_base + d_second
+    d_at = jnp.where(
+        d_chunk < 3.0, 16.0 * d_chunk + d_to, 48.0 + 5.0 * d_tile + d_row
+    )
+    d_there = (d_chunk < 3.0) | ((d_chunk < 9.0) & (d_row < 5.0))
+    d_pick = (iota((DP * 16, 64), 1) == d_at) & d_there
+    d_pick = jnp.where(d_pick, 1.0, 0.0).astype(BF16)
+
     for k in (1, 2, 3, 4):
         loads[k].wait()
     feat_right.wait_recv()
@@ -271,29 +302,17 @@
         total = fpad[at + 7 : at + 7 + step_rows, :] * tap[0]
         total = total + fpad[at + 8 : at + 8 + step_rows, :] * tap[1]
         total = total + fpad[at + 9 : at + 9 + step_rows, :] * tap[2]
-        emb[at : at + step_rows, :] = total.astype(BF16)
-    smoothed = emb[...]
-    act[...] = dot(smoothed, mix[...])
-    turned = smoothed.T
-    for k in range(NX):
-        for j in range(NZ):
-            at = k * XROWS + j * ZROWS
-            smooth[k, j] = turned[at : at + ZROWS]
-    smooth_copy = remote(smooth, smooth_in, S_SMOOTH, partner)
-    start(smooth_copy)
-
+        smooth_held[at : at + step_rows, :] = total.astype(BF16)
+    act[...] = dot(smooth_held[...], mix[...])
     root = math.sqrt(2.0 / math.pi)
 
     @pl.loop(0, ROWS // step_rows)
     def _(i):
         at = pl.ds(pl.multiple_of(i * step_rows, step_rows), step_rows)
         v = act[at, :]
-        sq = v * v
-        t = jnp.tanh(root * (v + 0.044715 * (sq * v)))
+        t = jnp.tanh(root * (v + 0.044715 * (v * v * v)))
+        bend[at, :] = t
         emb[at, :] = (0.5 * v * (1.0 + t)).astype(BF16)
-        act[at, :] = 0.5 * (1.0 + t) + (0.5 * root) * v * (1.0 - t * t) * (
-            1.0 + (3.0 * 0.044715) * sq
-        )
 
     for copy in code_copies:
         copy.wait_recv()
@@ -326,33 +345,23 @@
         start(copy)
 
     spread = hot[:both].T
-
-    z_place = iota((XROWS, 3 * TROWS), 0)
-    z_to = quotient(z_place, ZROWS)
-    z_chunk = z_place - ZROWS * z_to
-    z_tile = quotient(z_chunk, 5)
-    x_f = x.astype(F32)
-    z_f = z.astype(F32)
-    x_base = quotient(jnp.full((1, 1), 187.0) * x_f, 4)
-    z_row = quotient(187.0 * (NZ * x_f + z_to), 48) - x_base + (z_chunk - 5.0 * z_tile)
-    z_pick = (iota((XROWS, 3 * TROWS), 1) == z_tile * TROWS + z_row) & (z_chunk < 15.0)
-    z_pick = jnp.where(z_pick, 1.0, 0.0).astype(BF16)
-
-    d_place = iota((DP * 16, 64), 0)
-    d_to = quotient(d_place, 16)
-    d_chip = quotient(d_to, NC)
-    d_chunk = d_place - 16.0 * d_to
-    d_half = d_chunk - 3.0
-    d_second = jnp.where(d_half < 3.0, 0.0, 1.0)
-    d_tile = d_half - 3.0 * d_second
-    z_base = quotient(jnp.full((1, 1), 187.0) * seq_f, 48)
-    d_row = quotient(187.0 * (NY * seq_f + d_chip), 384) - z_base + d_second
-    d_at = jnp.where(
-        d_chunk < 3.0, 16.0 * d_chunk + d_to, 48.0 + 5.0 * d_tile + d_row
-    )
-    d_there = (d_chunk < 3.0) | ((d_chunk < 9.0) & (d_row < 5.0))
-    d_pick = (iota((DP * 16, 64), 1) == d_at) & d_there
-    d_pick = jnp.where(d_pick, 1.0, 0.0).astype(BF16)
+    turned = smooth_held[...].T
+    for k in range(NX):
+        for j in range(NZ):
+            at = k * XROWS + j * ZROWS
+            smooth[k, j] = turned[at : at + ZROWS]
+    smooth_copy = remote(smooth, smooth_in, S_SMOOTH, partner)
+    start(smooth_copy)
+
+
+    @pl.loop(0, ROWS // step_rows)
+    def _(i):
+        at = pl.ds(pl.multiple_of(i * step_rows, step_rows), step_rows)
+        v, t = act[at, :], bend[at, :]
+        act[at, :] = 0.5 * (1.0 + t) + (0.5 * root) * v * (1.0 - t * t) * (
+            1.0 + (3.0 * 0.044715) * (v * v)
+        )
+
 
     for copy in rows_copies:
         copy.wait_recv()
@@ -391,7 +400,7 @@
         xt_out[k] = head[core, base : base + TROWS, :].astype(BF16)
     xt_copies = {}
     for step in X_FAR:
-        to = lax.rem(x + step, NX)
+        to = wrapped(x + step, NX)
         xt_copies[step] = remote(
             xt_out.at[to], xt_in.at[step - 1], S_XT + step - 1, along_x(step)
         )
@@ -403,10 +412,10 @@
     pre_other = pre_in[...]
     xm_copies = {}
     for n, piece in enumerate(PIECES):
-        order = [lax.rem(x + step, NX) for step in (*X_FAR, 0)]
+        order = [wrapped(x + step, NX) for step in (*X_FAR, 0)]
         parts = [
             jnp.concatenate(
-                [source[to, lax.rem(z + step, NZ)] for to in order for step in piece], axis=0
+                [source[to, wrapped(z + step, NZ)] for to in order for step in piece], axis=0
             )
             for source in (smooth, smooth_in)
         ]
@@ -423,16 +432,6 @@
             xm_copies[n, step] = copy
         xm_own[n] = block[(NX - 1) * PROWS :]
 
-    slope_s = dot(pre[0], mix[:, :HALF], 1, 1) + dot(pre[1], mix[:, HALF:], 1, 1)
-    slope_s = slope_s.astype(BF16)
-    spad[8 : 8 + ROWS, :] = slope_s.astype(F32)
-    edge_out[0] = slope_s[ROWS - 16 :]
-    edge_out[1] = slope_s[:16]
-    edge_right = remote(edge_out.at[0], edge_in.at[0], S_SLOPE, along_seq(1))
-    edge_left = remote(edge_out.at[1], edge_in.at[1], S_SLOPE + 1, along_seq(-1))
-    start(edge_right)
-    start(edge_left)
-
     for step in X_NEAR:
         xt_copies[step].wait_recv()
     tail = xt_out[x].astype(F32)
@@ -446,7 +445,7 @@
 
     def t_copy(step):
         return remote(
-            t_out.at[lax.rem(z + step, NZ)], t_in.at[step - 1], S_T + step - 1, along_z(step)
+            t_out.at[wrapped(z + step, NZ)], t_in.at[step - 1], S_T + step - 1, along_z(step)
         )
 
     t_copies = {step: t_copy(step) for step in range(1, NZ)}
@@ -472,6 +471,16 @@
             start(z_copies[step])
 
     pass_on(0)
+
+    slope_s = dot(pre[0], mix[:, :HALF], 1, 1) + dot(pre[1], mix[:, HALF:], 1, 1)
+    slope_s = slope_s.astype(BF16)
+    spad[8 : 8 + ROWS, :] = slope_s.astype(F32)
+    edge_out[0] = slope_s[ROWS - 16 :]
+    edge_out[1] = slope_s[:16]
+    edge_right = remote(edge_out.at[0], edge_in.at[0], S_SLOPE, along_seq(1))
+    edge_left = remote(edge_out.at[1], edge_in.at[1], S_SLOPE + 1, along_seq(-1))
+    start(edge_right)
+    start(edge_left)
 
     depth = []
     for k in range(3):
@@ -585,7 +594,7 @@
 
     def d_copy(step):
         return remote(
-            d_out.at[lax.rem(dp + step, DP)], d_in.at[step - 1], S_Y + step - 1, along_dp(step)
+            d_out.at[wrapped(dp + step, DP)], d_in.at[step - 1], S_Y + step - 1, along_dp(step)
         )
 
     d_copies = {step: d_copy(step) for step in range(1, DP)}
@@ -693,6 +702,8 @@
             room(ROWS + 16, CH, dtype=F32),
             room(ROWS + 16, CH, dtype=F32),
             room(ROWS, CH, dtype=F32),
+            room(ROWS, CH, dtype=F32),
+            room(ROWS, CH),
             room(ROWS, CH),
             room(NX, NZ, ZROWS, ROWS),
             room(NX, NZ, ZROWS, ROWS),

time: 57.3 us -> 56.9 us (level)
  no operation moved by 1% of the time
where the time goes in v3:
time: 56.9 us; the launch traced here: 56.8 us
  Pallas kernels  55.5 us (98%)
  between operations  1.29 us (2%)
    pallas_call x1, Pallas kernels, on_device(): pl.pallas_call(body, out_shape=results, in_specs=[hbm] * 10, out_specs=(h...  53.6 us
    pallas_call x1, Pallas kernels, on_device(): pl.pallas_call(hand_over, out_shape=results[:2] + (jax.ShapeDtypeStruct((...  1.85 us

profile of v3, /device:TPU:1, one launch (start us, length us, event | category | flops | bytes accessed | tf_op | source)
XLA Modules:
  0.0 56.8 jit_solution(3024619774946140882)
XLA Ops:
  1.3 53.6 %shard_map.129 = (f32[64,184]{1,0:T(8,128)}, bf16[256,768]{1,0:T(8,128)(2,1)}, f32[1,768]{1,0:T(1,128)}, f32[1,187]{1,0:T(1,128)}) custom-call(bf16[256,768]{1,0:T(8,128)(2,1)} %bitcast.11, bf16[256,768]{1,0:T(8,128)(2,1)} %bitcast.12, bf16[3,768]{1,0:T(4,128)(2,1)} %refs_2_.1, bf16[768,768]{1,0:T(8,128)(2,1)} %refs_3_.1, bf16[184,768]{1,0:T(8,128)(2,1)} %refs_4_.1, ...), custom_call_target="tpu_custom_call" | custom-call | tf_op jit(solution)/shard_map/pallas_call | solution.py:685
  54.9 1.9 %shard_map.130 = (f32[64,184]{1,0:T(8,128)}, bf16[256,768]{1,0:T(8,128)(2,1)}, f32[768]{0:T(1024)}, f32[1,187]{1,0:T(1,128)}) custom-call(f32[64,184]{1,0:T(8,128)} %get-tuple-element.12.refs_0_, bf16[256,768]{1,0:T(8,128)(2,1)} %get-tuple-element.13.refs_1_, f32[1,768]{1,0:T(1,128)} %get-tuple-element.14.refs_2_, f32[1,187]{1,0:T(1,128)} %get-tuple-element.15.refs_3_), custom_call_target="tpu_custom_call" | custom-call | tf_op jit(solution)/shard_map/pallas_call | solution.py:764
